TPU v7x, 512 devices: a whole 4x8x8 slice. The times are simulated.
512 devices in a mesh: gx: 32 (over z, x), gy: 16 (over y, core).
Axes of the slice: x: 4, y: 8, z: 8, core: 2. Of those that a mesh axis runs over, the one named last changes fastest.
Arguments:
- probes: bfloat16 [48, 4, 512, 4096], P(None, None, 'gx', 'gy'), may hold values from -6 to 6
- classes: int32 [4, 512, 4096], P(None, 'gx', 'gy'), may hold values from 0 to 7
- class_table: float32 [8], replicated, may hold values from 0.3 to 3
- weights: float32 [4, 512, 4096], P(None, 'gx', 'gy'), may hold values from 5 to 500
- prior_block: float32 [4096, 256], P('gy'), may hold values from -0.1875 to 0.1875
- prior_left: float32 [8, 16, 4096], P(None, None, 'gy'), may hold values from -1.5 to 1.5
- prior_right: float32 [8, 16, 4096], P(None, None, 'gy'), may hold values from -6 to 6
- block_ranks: int32 [8], replicated, may hold values from 4 to 16
Outputs:
- basis: float32 [48, 4, 512, 4096], P(None, None, 'gx', 'gy')
- projected: float32 [48, 48], replicated
All inputs are finite; a program needn't handle non-finite values.
Results may differ from a plain program's by a relative error of at most 0.0018.
Values may be sent and summed in bfloat16 or wider, within the bound.
A program may use at most 64 MiB of HBM per device.

v0:
```python
import functools

import jax
import jax.numpy as jnp
from jax import lax
from jax.experimental import pallas as pl
from jax.experimental.pallas import tpu as pltpu
from jax.sharding import PartitionSpec as P

MESH = pl.DeviceIdType.MESH
HIGH = lax.Precision.HIGHEST
F32 = jnp.float32
BF16 = jnp.bfloat16
LANES = 128
VMEM = pl.BlockSpec(memory_space=pltpu.VMEM)
SMEM = pl.BlockSpec(memory_space=pltpu.SMEM)
ANY = pl.BlockSpec(memory_space=pl.ANY)
NT = (((1,), (1,)), ((), ()))


def signal_all(devices):
    barrier = pltpu.get_barrier_semaphore()
    for device in devices:
        pl.semaphore_signal(barrier, inc=1, device_id=device, device_id_type=MESH)
    return barrier, len(devices)


def remote(src, dst, send, recv, device):
    copy = pltpu.make_async_remote_copy(
        src_ref=src, dst_ref=dst, send_sem=send, recv_sem=recv, device_id=device, device_id_type=MESH
    )
    copy.start()
    return copy


def halo_kernel(
    ng, ny, k, nz, nx,
    probes, classes, table, weights,
    pt, xh, hy, cx, cy, cond,
    pf, hs, cxs, cys, send_sem, recv_sem,
):
    gx, gy = lax.axis_index("gx"), lax.axis_index("gy")
    east, west = lax.rem(gx + 1, ng), lax.rem(gx + ng - 1, ng)
    north, south = lax.rem(gy + 1, ny), lax.rem(gy + ny - 1, ny)
    around = [(west, gy), (east, gy)]
    for column in (south, north):
        for row in (west, gx, east):
            around.append((row, column))
    barrier, count = signal_all(around)

    lines = nz * nx
    chunk = 512

    def widen(i, carry):
        rows = pl.ds(pl.multiple_of(i * chunk, chunk), chunk)
        value = probes[rows, :].astype(F32)
        pf[0, rows, :] = value[:, :LANES]
        pf[1, rows, :] = value[:, LANES:]
        return carry

    lax.fori_loop(0, k * lines // chunk, widen, 0)

    for z in range(nz):
        picked = classes[z]
        value = jnp.zeros(picked.shape, F32)
        for index in range(table.shape[0]):
            value = jnp.where(picked == index, table[index], value)
        cond[z] = value
        cxs[0, 4 * z : 4 * z + 3, :] = value[0:3, :]
        cxs[1, 4 * z : 4 * z + 3, :] = value[nx - 3 : nx, :]
        cxs[0, 4 * z + 3 : 4 * z + 4, :] = weights[z, 0:1, :]
        cxs[1, 4 * z + 3 : 4 * z + 4, :] = weights[z, nx - 1 : nx, :]
    lane = lax.broadcasted_iota(jnp.int32, (nx, LANES), 1)
    low = jnp.zeros((nx, LANES), F32)
    high = jnp.zeros((nx, LANES), F32)
    for z in range(nz):
        here = lane // 4 == z
        last = lane % 4 == 3
        first_tile, last_tile = cond[z, :, :LANES], cond[z, :, LANES:]
        w_first, w_last = weights[z, :, :LANES], weights[z, :, LANES:]
        own = jnp.where(last, pltpu.roll(w_first, 4 * z + 3, 1), pltpu.roll(first_tile, 4 * z, 1))
        low = jnp.where(here, own, low)
        own = jnp.where(last, pltpu.roll(w_last, 4 * z + 4, 1), pltpu.roll(last_tile, 4 * z + 3, 1))
        high = jnp.where(here, own, high)
    cys[0] = low
    cys[1] = high

    def turn(line):
        lo = pf[0, pl.ds(line, k, stride=lines), :]
        hi = pf[1, pl.ds(line, k, stride=lines), :]
        pt[line // nx, lax.rem(line, nx)] = jnp.concatenate([lo, hi], axis=1).astype(BF16)
        return lo, hi

    place = lax.broadcasted_iota(jnp.int32, (k, LANES), 1) // 2

    def edge_of(line, carry):
        low, high = carry
        lo, hi = turn(line)
        low = jnp.where(place == line, pltpu.roll(lo, 2 * line, 1), low)
        high = jnp.where(place == line, pltpu.roll(hi, lax.rem(2 * line + 2, LANES), 1), high)
        return low, high

    def outer(i, carry):
        part = lax.rem(i, 4)
        return edge_of((i // 4) * nx + jnp.where(part < 2, part, nx - 4 + part), carry)

    def inner(i, carry):
        return edge_of((i // (nx - 4)) * nx + 2 + lax.rem(i, nx - 4), carry)

    zero = jnp.zeros((k, LANES), F32)
    carry = lax.fori_loop(0, nz * 4, outer, (zero, zero))
    pl.semaphore_wait(barrier, count)
    copies = [
        remote(pt.at[:, nx - 2 : nx], xh.at[0], send_sem.at[0], recv_sem.at[0], (east, gy)),
        remote(pt.at[:, 0:2], xh.at[1], send_sem.at[1], recv_sem.at[1], (west, gy)),
        remote(cxs.at[1], cx.at[0], send_sem.at[2], recv_sem.at[2], (east, gy)),
        remote(cxs.at[0], cx.at[1], send_sem.at[3], recv_sem.at[3], (west, gy)),
    ]
    low, high = lax.fori_loop(0, nz * (nx - 4), inner, carry)
    hs[0] = low.astype(BF16)
    hs[1] = high.astype(BF16)
    used = 4
    for side, column in ((0, north), (1, south)):
        for which, row in ((2, west), (1, gx), (0, east)):
            slot = side * 3 + which
            source = 1 - side
            copies.append(
                remote(hs.at[source], hy.at[slot], send_sem.at[used], recv_sem.at[used], (row, column))
            )
            copies.append(
                remote(
                    cys.at[source], cy.at[slot], send_sem.at[used + 1], recv_sem.at[used + 1], (row, column)
                )
            )
            used += 2
    for copy in copies:
        copy.wait()


def sketch_kernel(
    ng, ny, k, nz, nx, levels, leaf,
    pt, xh, hy, cx, cy, cond, weights, block, left, right, ranks,
    shl, gram, leafpart, uc,
    ce, dg, dd, wd, fx, fyp, fym, fz, f1, a1, wt, acc, cuf,
):
    gx, gy = lax.axis_index("gx"), lax.axis_index("gy")
    has_west = (gx > 0).astype(F32)
    has_east = (gx < ng - 1).astype(F32)
    has_south = (gy > 0).astype(F32)
    has_north = (gy < ny - 1).astype(F32)
    has_x = (has_west, 1.0, has_east)
    has_y = (has_south, has_north)
    rank = left.shape[1]

    wt[0:leaf, :] = block[...].astype(BF16)
    row = lax.broadcasted_iota(jnp.int32, (rank, leaf), 0)
    for level in range(levels):
        gain = jnp.where(row < ranks[level], float(leaf * 2**level) ** -0.5, 0.0)
        at = leaf + 2 * level * rank
        wt[at : at + rank, :] = (right[level] * gain).astype(BF16)
        wt[at + rank : at + 2 * rank, :] = left[level].astype(BF16)

    tall = nx + 16
    wide = 3 * LANES
    lane = lax.broadcasted_iota(jnp.int32, (nx, LANES), 1)
    for z in range(nz):
        ce[z] = jnp.zeros((tall, wide), F32)
        wd[z] = jnp.zeros((tall, wide), F32)
        ce[z, 8 : 8 + nx, 0 : 2 * LANES] = cond[z]
        wd[z, 8 : 8 + nx, 0 : 2 * LANES] = weights[z]
        ce[z, 5:8, 0 : 2 * LANES] = cx[0, 4 * z : 4 * z + 3, :] * has_west
        wd[z, 7:8, 0 : 2 * LANES] = cx[0, 4 * z + 3 : 4 * z + 4, :] * has_west
        ce[z, 8 + nx : 11 + nx, 0 : 2 * LANES] = cx[1, 4 * z : 4 * z + 3, :] * has_east
        wd[z, 8 + nx : 9 + nx, 0 : 2 * LANES] = cx[1, 4 * z + 3 : 4 * z + 4, :] * has_east
        for which in range(3):
            above = cy[3 + which] * (has_x[which] * has_y[1])
            below = cy[which] * (has_x[which] * has_y[0])
            value = jnp.where(lane < 3, pltpu.roll(above, (LANES - 4 * z) % LANES, 1), 0.0)
            value = jnp.where(lane > LANES - 4, pltpu.roll(below, LANES - 3 - 4 * z, 1), value)
            if which == 0:
                ce[z, 0:8, 2 * LANES :] = value[nx - 8 :, :]
            elif which == 2:
                ce[z, 8 + nx :, 2 * LANES :] = value[:8, :]
            else:
                ce[z, 8 : 8 + nx, 2 * LANES :] = value
                value = jnp.where(lane == 0, pltpu.roll(above, LANES - 3 - 4 * z, 1), 0.0)
                value = jnp.where(lane == LANES - 1, pltpu.roll(below, LANES - 4 - 4 * z, 1), value)
                wd[z, 8 : 8 + nx, 2 * LANES :] = value
    for z in range(nz):
        centre = ce[z]
        upper = ce[z + 1] if z + 1 < nz else jnp.zeros_like(centre)
        lower = ce[z - 1] if z > 0 else jnp.zeros_like(centre)
        face_x = 0.5 * (centre + pltpu.roll(centre, tall - 1, 0))
        face_y = 0.5 * (centre + pltpu.roll(centre, wide - 1, 1))
        back_y = pltpu.roll(face_y, 1, 1)
        face_z = 0.5 * (centre + upper)
        total = 1.0 + face_x + pltpu.roll(face_x, 1, 0) + face_y + back_y
        total = total + face_z + 0.5 * (centre + lower)
        inverse = 1.0 / total
        fx[z] = face_x
        fyp[z] = face_y
        fym[z] = back_y
        fz[z] = face_z
        dg[z] = total
        dd[z] = inverse
        wd[z] = wd[z] * inverse

    tile_lane = lax.broadcasted_iota(jnp.int32, (k, LANES), 1)

    def tiles(ref, z, x):
        whole = ref[z, pl.ds(x + 8, 1), :]
        return [whole[:, i * LANES : (i + 1) * LANES] for i in range(3)]

    def split(value):
        return [value[:, i * LANES : (i + 1) * LANES] for i in range(value.shape[1] // LANES)]

    def store(ref, z, x, parts):
        for i in range(len(parts)):
            ref[z, x, :, i * LANES : (i + 1) * LANES] = parts[i]

    def edge_tile(z, x, which):
        line = z * nx + x
        above = hy[3 + which].astype(F32) * (has_x[which] * has_y[1])
        below = hy[which].astype(F32) * (has_x[which] * has_y[0])
        above = pltpu.roll(above, lax.rem(LANES - 2 * line + LANES, LANES), 1)
        below = pltpu.roll(below, lax.rem(2 * LANES - 2 - 2 * line, LANES), 1)
        value = jnp.where(tile_lane < 2, above, 0.0)
        return jnp.where(tile_lane >= LANES - 2, below, value)

    def forward(z, x, value, edge):
        inverse = tiles(dd, z, x)
        parts = split(value) + [edge]
        store(f1, z, x + 2, [parts[i] * inverse[i] for i in range(3)])

    def forward_inner(x, carry):
        for z in range(nz):
            forward(z, x, pt[z, x].astype(F32), edge_tile(z, x, 1))
        return carry

    lax.fori_loop(0, nx, forward_inner, 0)
    for z in range(nz):
        for i in range(2):
            forward(z, i - 2, xh[0, z, i].astype(F32) * has_west, edge_tile(z, nx - 2 + i, 0))
            forward(z, nx + i, xh[1, z, i].astype(F32) * has_east, edge_tile(z, i, 2))

    def near(ref, z, x, row, count):
        centre = split(ref[z, row])
        ahead = [pltpu.roll(part, LANES - 1, 1) for part in centre]
        behind = [pltpu.roll(part, 1, 1) for part in centre]
        east, west = split(ref[z, row + 1]), split(ref[z, row - 1])
        face_e, face_w = tiles(fx, z, x), tiles(fx, z, x - 1)
        face_n, face_s = tiles(fyp, z, x), tiles(fym, z, x)
        if z + 1 < nz:
            upper, face_u = split(ref[z + 1, row]), tiles(fz, z, x)
        if z > 0:
            lower, face_d = split(ref[z - 1, row]), tiles(fz, z - 1, x)
        sums = []
        for i in range(count):
            north = jnp.where(tile_lane == LANES - 1, ahead[(i + 1) % 3], ahead[i])
            south = jnp.where(tile_lane == 0, behind[(i + 2) % 3], behind[i])
            total = face_e[i] * east[i] + face_w[i] * west[i]
            total = total + (face_n[i] * north + face_s[i] * south)
            if z + 1 < nz:
                total = total + face_u[i] * upper[i]
            if z > 0:
                total = total + face_d[i] * lower[i]
            sums.append(total)
        return centre, sums

    def adjoint(i, carry):
        x = i - 1
        for z in range(nz):
            centre, sums = near(f1, z, x, x + 2, 3)
            diagonal, inverse, gain = tiles(dg, z, x), tiles(dd, z, x), tiles(wd, z, x)
            parts = [
                (centre[i] * diagonal[i] + sums[i]) * gain[i] * inverse[i] for i in range(3)
            ]
            store(a1, z, x + 1, parts)
        return carry

    lax.fori_loop(0, nx + 2, adjoint, 0)

    acc[...] = jnp.zeros_like(acc)

    def finish(x, carry):
        whole_high, whole_low = [], []
        for z in range(nz):
            centre, sums = near(a1, z, x, x + 1, 2)
            diagonal, inverse = tiles(dg, z, x), tiles(dd, z, x)
            source = split(pt[z, x].astype(F32))
            sketch = jnp.concatenate(
                [
                    (centre[i] * diagonal[i] + sums[i]) * inverse[i] + source[i]
                    for i in range(2)
                ],
                axis=1,
            )
            high = sketch.astype(BF16)
            low = (sketch - high.astype(F32)).astype(BF16)
            shl[z * nx + x, 0:k, :] = high
            shl[z * nx + x, k : 2 * k, :] = low
            whole_high.append(high)
            whole_low.append(low)
        applied = lax.dot_general(
            jnp.concatenate(whole_high, axis=0), wt[...], NT, preferred_element_type=F32
        )
        rows = []
        for z in range(nz):
            part = applied[z * k : (z + 1) * k]
            cuf[z * nx + x] = part[:, leaf:]
            rows.append(part[:, :leaf].astype(BF16))
        high = jnp.concatenate(whole_high, axis=1)
        low = jnp.concatenate(whole_low, axis=1)
        lhs = jnp.concatenate([high, low], axis=0)
        rhs = jnp.concatenate([high, low, jnp.concatenate(rows, axis=1)], axis=0)
        acc[...] += lax.dot_general(lhs, rhs, NT, preferred_element_type=F32)
        return carry

    lax.fori_loop(0, nx, finish, 0)

    pad = jnp.zeros((k, LANES - k), F32)
    value = acc[...]
    total = value[0:k, 0:k] + (value[0:k, k : 2 * k] + value[k : 2 * k, 0:k]) + value[k:, k : 2 * k]
    gram[...] = jnp.concatenate([total, pad], axis=1)
    total = value[0:k, 2 * k :] + value[k:, 2 * k :]
    leafpart[...] = jnp.concatenate([total, pad], axis=1)

    count = LANES // rank
    slot = tile_lane // rank

    def gather(group, carry):
        parts = [cuf[group * count + j] for j in range(count)]
        step = 1
        while step < count:
            bit = (slot // step) % 2 == 0
            for i in range(count):
                if (i // step) % 2 == 0:
                    one, two = parts[i], parts[i + step]
                    parts[i] = jnp.where(bit, one, pltpu.roll(two, step * rank, 1))
                    parts[i + step] = jnp.where(bit, pltpu.roll(one, LANES - step * rank, 1), two)
            step *= 2
        for index in range(2 * levels):
            uc[index, group] = parts[index].astype(BF16)
        return carry

    lax.fori_loop(0, nz * nx // count, gather, 0)


def reduce_kernel(
    ng, ny, k, levels, groups, cells,
    gram, leafpart, uc,
    linv, projected,
    pieces, rs, sums, ar, totals, ag, trees, sems,
):
    gx, gy = lax.axis_index("gx"), lax.axis_index("gy")
    rows = k // ny
    column = [lax.rem(gy + d, ny) for d in range(1, ny)]
    across = [lax.rem(gx + d, ng) for d in range(1, ng)]
    barrier, count = signal_all([(gx, e) for e in column] + [(e, gy) for e in across])
    send_sem, recv_sem, tree_send, tree_recv = sems

    def scatter(which, value):
        for i in range(k):
            pieces[which, i // rows, i % rows, :] = value[i, :]
        rs[which, gy] = pieces[which, gy]
        return [
            remote(
                pieces.at[which, e], rs.at[which, gy],
                send_sem.at[which, 0, d], recv_sem.at[which, 0, d], (gx, e),
            )
            for d, e in enumerate(column)
        ]

    def added(ref, which, count):
        parts = [ref[which, i] for i in range(count)]
        while len(parts) > 1:
            parts = [
                parts[i] + parts[i + 1] if i + 1 < len(parts) else parts[i]
                for i in range(0, len(parts), 2)
            ]
        return parts[0]

    def exchange(which, copies):
        for copy in copies:
            copy.wait()
        sums[which] = added(rs, which, ny)
        ar[which, gx] = sums[which]
        return [
            remote(
                sums.at[which], ar.at[which, gx],
                send_sem.at[which, 1, d], recv_sem.at[which, 1, d], (e, gy),
            )
            for d, e in enumerate(across)
        ]

    def spread(which, copies):
        for copy in copies:
            copy.wait()
        totals[which] = added(ar, which, ng)
        ag[which, gy] = totals[which]
        return [
            remote(
                totals.at[which], ag.at[which, gy],
                send_sem.at[which, 2, d], recv_sem.at[which, 2, d], (gx, e),
            )
            for d, e in enumerate(column)
        ]

    def collect(which, copies):
        for copy in copies:
            copy.wait()
        parts = [ag[which, i // rows, i % rows : i % rows + 1, :] for i in range(k)]
        return jnp.concatenate(parts, axis=0) * (1.0 / cells)

    pl.semaphore_wait(barrier, count)
    flight = scatter(0, gram[...])

    def flipped(bits):
        device = gy
        for b in range(levels):
            if bits >> b & 1:
                device = device + (1 - 2 * lax.rem(device // 2**b, 2)) * 2**b
        return device

    tree = []
    for level in range(levels):
        half = 2**level
        share = groups // half
        for bits in range(1, 2 * half):
            peer = flipped(bits)
            kind = 2 * level + (1 if bits < half else 0)
            begin = lax.rem(peer, half) * share
            tree.append(
                remote(
                    uc.at[kind, pl.ds(begin, share)], trees[level].at[bits - 1],
                    tree_send.at[2 * half - 2 - level + bits], tree_recv.at[2 * half - 2 - level + bits],
                    (gx, peer),
                )
            )

    flight = exchange(0, flight)
    for copy in tree:
        copy.wait()
    total = leafpart[:, 0:k]
    for level in range(levels):
        half = 2**level
        share = groups // half
        begin = lax.rem(gy, half) * share
        for j in range(share):
            own = uc[2 * level + 1, begin + j].astype(F32)
            for bits in range(1, half):
                own = own + trees[level][bits - 1, j].astype(F32)
            other = trees[level][half - 1, j].astype(F32)
            for bits in range(half + 1, 2 * half):
                other = other + trees[level][bits - 1, j].astype(F32)
            total = total + lax.dot_general(
                own.astype(BF16), other.astype(BF16), NT, preferred_element_type=F32
            )
    total = jnp.concatenate([total, jnp.zeros((k, LANES - k), F32)], axis=1)
    flight = spread(0, flight)
    second = scatter(1, total)
    matrix = collect(0, flight)

    row = lax.broadcasted_iota(jnp.int32, (k, LANES), 0)
    lane = lax.broadcasted_iota(jnp.int32, (k, LANES), 1)
    start = LANES // 2
    whole = jnp.where(lane < k, matrix, jnp.where(lane == row + start, 1.0, 0.0))
    blocks = [whole[8 * t : 8 * t + 8] for t in range(k // 8)]
    inner = lax.broadcasted_iota(jnp.int32, (8, LANES), 0)
    for j in range(k):
        t, s = divmod(j, 8)
        pivot_row = blocks[t][s : s + 1, :]
        scaled = pivot_row * (1.0 / pivot_row[:, j : j + 1])
        for i in range(t, k // 8):
            factor = blocks[i][:, j : j + 1]
            change = factor * scaled
            if i == t:
                change = jnp.where(inner > s, change, 0.0)
            blocks[i] = blocks[i] - change
        if j == k // 3:
            second = exchange(1, second)
        if j == k - k // 6:
            second = spread(1, second)
    whole = jnp.concatenate(blocks, axis=0)
    pivots = jnp.sum(jnp.where(lane == row, whole, 0.0), axis=1, keepdims=True)
    inverse = whole[:, start : start + k] / jnp.sqrt(pivots)
    linv[...] = inverse
    middle = collect(1, second)[:, 0:k]
    product = jnp.dot(inverse, middle, precision=HIGH, preferred_element_type=F32)
    product = lax.dot_general(product, inverse, NT, precision=HIGH, preferred_element_type=F32)
    projected[...] = product + jnp.where(lane[:, 0:k] == row[:, 0:k], 1.0, 0.0)


def basis_kernel(k, nz, nx, shl, linv, out, buffer, sem):
    inverse = linv[...]
    high = inverse.astype(BF16)
    low = (inverse - high.astype(F32)).astype(BF16)
    lhs = jnp.concatenate(
        [
            jnp.concatenate([high, high], axis=1),
            jnp.concatenate([low, jnp.zeros_like(low)], axis=1),
        ],
        axis=0,
    )
    copies = []
    for z in range(nz):

        def one(x, carry):
            value = jnp.dot(lhs, shl[z * nx + x], preferred_element_type=F32)
            value = value[0:k] + value[k:]
            buffer[z, 0, pl.ds(x, k, stride=nx), :] = value[:, :LANES]
            buffer[z, 1, pl.ds(x, k, stride=nx), :] = value[:, LANES:]
            return carry

        lax.fori_loop(0, nx, one, 0, unroll=4)
        for i in range(2):
            copy = pltpu.make_async_copy(
                buffer.at[z, i].reshape(k, nx, LANES),
                out.at[:, z, :, i * LANES : (i + 1) * LANES],
                sem.at[z, i],
            )
            copy.start()
            copies.append(copy)
    for copy in copies:
        copy.wait()


def params(**more):
    return pltpu.CompilerParams(vmem_limit_bytes=40 * 2**20, **more)


def shards(
    probes, classes, class_table, weights, prior_block, prior_left, prior_right, block_ranks
):
    ng, ny = lax.axis_size("gx"), lax.axis_size("gy")
    k, nz, nx, leaf = probes.shape
    levels = ny.bit_length() - 1
    rank = prior_left.shape[1]
    lines = nz * nx
    groups = lines * rank // LANES
    cells = float(nz * nx * leaf * ng * ny)
    shape = jax.ShapeDtypeStruct
    dma = pltpu.SemaphoreType.DMA

    pt, xh, hy, cx, cy, cond = pl.pallas_call(
        functools.partial(halo_kernel, ng, ny, k, nz, nx),
        out_shape=(
            shape((nz, nx, k, leaf), BF16),
            shape((2, nz, 2, k, leaf), BF16),
            shape((6, k, LANES), BF16),
            shape((2, 4 * nz, leaf), F32),
            shape((6, nx, LANES), F32),
            shape((nz, nx, leaf), F32),
        ),
        in_specs=[VMEM, VMEM, SMEM, VMEM],
        out_specs=(VMEM,) * 6,
        scratch_shapes=[
            pltpu.VMEM((2, k * lines, LANES), F32),
            pltpu.VMEM((2, k, LANES), BF16),
            pltpu.VMEM((2, 4 * nz, leaf), F32),
            pltpu.VMEM((2, nx, LANES), F32),
            dma((16,)),
            dma((16,)),
        ],
        compiler_params=params(collective_id=0, has_side_effects=True),
    )(probes.reshape(k * lines, leaf), classes, class_table, weights)

    field = pltpu.VMEM((nz, nx + 16, 3 * LANES), F32)
    shl, gram, leafpart, uc = pl.pallas_call(
        functools.partial(sketch_kernel, ng, ny, k, nz, nx, levels, leaf),
        out_shape=(
            shape((lines, 2 * k, leaf), BF16),
            shape((k, LANES), F32),
            shape((k, LANES), F32),
            shape((2 * levels, groups, k, LANES), BF16),
        ),
        in_specs=[VMEM] * 10 + [SMEM],
        out_specs=(VMEM,) * 4,
        scratch_shapes=[field] * 8
        + [
            pltpu.VMEM((nz, nx + 4, k, 3 * LANES), F32),
            pltpu.VMEM((nz, nx + 2, k, 3 * LANES), F32),
            pltpu.VMEM((leaf + LANES, leaf), BF16),
            pltpu.VMEM((2 * k, 3 * k), F32),
            pltpu.VMEM((lines, k, LANES), F32),
        ],
        compiler_params=params(),
    )(
        pt, xh, hy, cx, cy, cond, weights, prior_block, prior_left[:levels],
        prior_right[:levels], block_ranks,
    )

    rows = k // ny
    edges = 2 * ny
    linv, projected = pl.pallas_call(
        functools.partial(reduce_kernel, ng, ny, k, levels, groups, cells),
        out_shape=(shape((k, k), F32), shape((k, k), F32)),
        in_specs=[VMEM] * 3,
        out_specs=(VMEM, VMEM),
        scratch_shapes=[
            pltpu.VMEM((2, ny, rows, LANES), F32),
            pltpu.VMEM((2, ny, rows, LANES), F32),
            pltpu.VMEM((2, rows, LANES), F32),
            pltpu.VMEM((2, ng, rows, LANES), F32),
            pltpu.VMEM((2, rows, LANES), F32),
            pltpu.VMEM((2, ny, rows, LANES), F32),
            [
                pltpu.VMEM((2 ** (level + 1) - 1, groups >> level, k, LANES), BF16)
                for level in range(levels)
            ],
            [
                dma((2, 3, max(ny, ng))),
                dma((2, 3, max(ny, ng))),
                dma((edges,)),
                dma((edges,)),
            ],
        ],
        compiler_params=params(collective_id=1, has_side_effects=True),
    )(gram, leafpart, uc)

    basis = pl.pallas_call(
        functools.partial(basis_kernel, k, nz, nx),
        out_shape=shape((k, nz, nx, leaf), F32),
        in_specs=[VMEM, VMEM],
        out_specs=ANY,
        scratch_shapes=[
            pltpu.VMEM((nz, 2, k * nx, LANES), F32),
            dma((nz, 2)),
        ],
        compiler_params=params(),
    )(shl, linv)
    return basis, projected


def solution(mesh):
    return jax.shard_map(
        shards,
        mesh=mesh,
        in_specs=(
            P(None, None, "gx", "gy"),
            P(None, "gx", "gy"),
            P(),
            P(None, "gx", "gy"),
            P("gy", None),
            P(None, None, "gy"),
            P(None, None, "gy"),
            P(),
        ),
        out_specs=(P(None, None, "gx", "gy"), P()),
        check_vma=False,
    )
```

profile of v0, /device:TPU:1, one launch (start us, length us, event | category | flops | bytes accessed | tf_op | source)
XLA Modules:
  0.0 100.5 jit_solution(11522517787040542517)
XLA Ops:
  0.6 0.8 slice.6.left
  1.5 0.8 slice.7.right
  2.3 0.0 copy-start
  2.3 1.4 %copy-done = bf16[48,4,16,256]{3,2,1,0:T(8,128)(2,1)S(1)} copy-done((bf16[48,4,16,256]{3,2,1,0:T(8,128)(2,1)S(1)}, bf16[48,4,16,256]{3,2,1,0:T(8,128)(2,1)}, u32[]{:S(2)}) %copy-start) | copy-done | bytes 1572888
  3.7 0.0 copy-start.2
  3.7 0.8 copy-done.2
  4.6 0.0 copy-start.3
  4.6 0.8 copy-done.3
  5.4 0.0 copy-start.4
  5.4 0.7 copy-done.4
  6.1 25.0 %shard_map.95 = (bf16[4,16,48,256]{3,2,1,0:T(8,128)(2,1)S(1)}, bf16[2,4,2,48,256]{4,3,2,1,0:T(8,128)(2,1)S(1)}, bf16[6,48,128]{2,1,0:T(8,128)(2,1)S(1)}, f32[2,1...) custom-call(bf16[3072,256]{1,0:T(8,128)(2,1)S(1)} %bitcast.1, ...), custom_call_target="tpu_custom_call" | custom-call | tf_op jit(solution)/shard_map/pallas_call | solution.py:545
  31.1 0.0 copy-start.1
  31.1 0.9 copy-done.1
  32.0 0.0 copy-start.5
  32.0 0.7 copy-done.5
  32.7 18.1 %shard_map.96 = (bf16[64,96,256]{2,1,0:T(8,128)(2,1)S(1)}, f32[48,128]{1,0:T(8,128)S(1)}, f32[48,128]{1,0:T(8,128)S(1)}, bf16[8,8,48,128]{3,2,1,0:T(8,128)(2,1)S(1)}) custom-call(bf16[4,16,48,256]{3,2,1,0:T(8,128)(2,1)S(1)} %get-tuple-element.14.pt, bf16[2,4,2,48,256]{4,3,2,1,0:T(8,128)(2,1)S(1)} %get-tuple-element.15.xh, ...), custom_call_target="tpu_custom_call" | custom-call | tf_op jit(solution)/shard_map/pallas_call | solution.py:569
  50.8 44.5 %shard_map.97 = (f32[48,48]{1,0:T(8,128)S(1)}, f32[48,48]{1,0:T(8,128)S(1)}) custom-call(f32[48,128]{1,0:T(8,128)S(1)} %get-tuple-element.21.gram, f32[48,128]{1,0:T(8,128)S(1)} %get-tuple-element.22.leafpart, bf16[8,8,48,128]{3,2,1,0:T(8,128)(2,1)S(1)} %get-tuple-element.23.uc), custom_call_target="tpu_custom_call" | custom-call | tf_op jit(solution)/shard_map/pallas_call | solution.py:595
  95.3 4.5 %shard_map.98 = f32[48,4,16,256]{3,2,1,0:T(8,128)} custom-call(bf16[64,96,256]{2,1,0:T(8,128)(2,1)S(1)} %get-tuple-element.20.shl, f32[48,48]{1,0:T(8,128)S(1)} %get-tuple-element.24.linv), custom_call_target="tpu_custom_call" | custom-call | tf_op jit(solution)/shard_map/pallas_call | solution.py:621
  99.8 0.6 copy.11
Async XLA Ops:
  2.3 1.4 %copy-start = (bf16[48,4,16,256]{3,2,1,0:T(8,128)(2,1)S(1)}, bf16[48,4,16,256]{3,2,1,0:T(8,128)(2,1)}, u32[]{:S(2)}) copy-start(bf16[48,4,16,256]{3,2,1,0:T(8,128)(2,1)} %param.8) | copy-start | bytes 4718596
  3.7 0.8 copy-start.2
  4.6 0.8 copy-start.3
  5.4 0.7 copy-start.4
  31.1 1.0 copy-start.1
  32.0 0.7 copy-start.5
where the time goes:
time: 101 us; the launch traced here: 100 us
  Pallas kernels  92.1 us (91%)
  local copies, waits for them, and re-layouts  7.64 us (8%)
    pallas_call x1, Pallas kernels, shards(): pl.pallas_call(functools.partial(reduce_kernel, ng, ny, k, levels, groups...  44.5 us
    pallas_call x1, Pallas kernels, shards(): pl.pallas_call(functools.partial(halo_kernel, ng, ny, k, nz, nx), out_sha...  25 us
    pallas_call x1, Pallas kernels, shards(): pl.pallas_call(functools.partial(sketch_kernel, ng, ny, k, nz, nx, levels...  18.1 us
    unnamed x13, local copies, waits for them, and re-layouts  5.95 us
    pallas_call x1, Pallas kernels, shards(): pl.pallas_call(functools.partial(basis_kernel, k, nz, nx), out_shape=shap...  4.52 us

commit v1 on v0

--- a/solution.py
+++ b/solution.py
@@ -15,6 +15,7 @@
 VMEM = pl.BlockSpec(memory_space=pltpu.VMEM)
 SMEM = pl.BlockSpec(memory_space=pltpu.SMEM)
 ANY = pl.BlockSpec(memory_space=pl.ANY)
+HBM = pl.BlockSpec(memory_space=pltpu.HBM)
 NT = (((1,), (1,)), ((), ()))
 
 
@@ -33,11 +34,14 @@
     return copy
 
 
-def halo_kernel(
-    ng, ny, k, nz, nx,
-    probes, classes, table, weights,
-    pt, xh, hy, cx, cy, cond,
-    pf, hs, cxs, cys, send_sem, recv_sem,
+def sketch_kernel(
+    ng, ny, k, nz, nx, levels, leaf, groups, cells,
+    probes_in, classes_in, table_in, weights_in, block_in, left_in, right_in, ranks_in,
+    shl_out, small_out,
+    shl, small, store_sem, probes, classes, table, weights, block, left, right, ranks, load_sem,
+    pt, cond, pf, xh, hy, cx, cy, hs, cxs, cys, send_sem, recv_sem,
+    ce, dg, dd, wd, fx, fyp, fym, fz, f1, a1, wt, acc, cuf, uc,
+    trees, tree_send, tree_recv, packed, gathered, sum_send, sum_recv,
 ):
     gx, gy = lax.axis_index("gx"), lax.axis_index("gy")
     east, west = lax.rem(gx + 1, ng), lax.rem(gx + ng - 1, ng)
@@ -46,19 +50,49 @@
     for column in (south, north):
         for row in (west, gx, east):
             around.append((row, column))
-    barrier, count = signal_all(around)
+
+    across, pair = min(4, ng), min(2, ny)
+    deep, high_y = ng // across, ny // pair
+    at_z, at_x = gx // across, lax.rem(gx, across)
+    at_y, at_c = gy // pair, lax.rem(gy, pair)
+    stages = [
+        (
+            [
+                (
+                    at_z * across + lax.rem(at_x + d % across, across),
+                    at_y * pair + lax.rem(at_c + d // across, pair),
+                )
+                for d in range(1, across * pair)
+            ],
+            at_c * across + at_x,
+        ),
+        ([(gx, lax.rem(at_y + d, high_y) * pair + at_c) for d in range(1, high_y)], at_y),
+        ([(lax.rem(at_z + d, deep) * across + at_x, gy) for d in range(1, deep)], at_z),
+    ]
+    column = [(gx, lax.rem(gy + d, ny)) for d in range(1, ny)]
+    barrier, count = signal_all(around + stages[0][0] + stages[2][0] + column)
+
+    loads = [
+        pltpu.make_async_copy(source, target, load_sem.at[i])
+        for i, (source, target) in enumerate(
+            [
+                (classes_in, classes),
+                (weights_in, weights),
+                (table_in, table),
+                (probes_in, probes),
+                (block_in, block),
+                (left_in.at[0:levels], left),
+                (right_in.at[0:levels], right),
+                (ranks_in, ranks),
+            ]
+        )
+    ]
+    for load in loads:
+        load.start()
 
     lines = nz * nx
-    chunk = 512
-
-    def widen(i, carry):
-        rows = pl.ds(pl.multiple_of(i * chunk, chunk), chunk)
-        value = probes[rows, :].astype(F32)
-        pf[0, rows, :] = value[:, :LANES]
-        pf[1, rows, :] = value[:, LANES:]
-        return carry
-
-    lax.fori_loop(0, k * lines // chunk, widen, 0)
+    for load in loads[:3]:
+        load.wait()
 
     for z in range(nz):
         picked = classes[z]
@@ -85,65 +119,65 @@
     cys[0] = low
     cys[1] = high
 
-    def turn(line):
+    loads[3].wait()
+    chunk = 512
+
+    def widen(i, carry):
+        rows = pl.ds(pl.multiple_of(i * chunk, chunk), chunk)
+        value = probes[rows, :].astype(F32)
+        pf[0, rows, :] = value[:, :LANES]
+        pf[1, rows, :] = value[:, LANES:]
+        return carry
+
+    lax.fori_loop(0, k * lines // chunk, widen, 0)
+
+    place = lax.broadcasted_iota(jnp.int32, (k, LANES), 1) // 2
+
+    def turn(line, carry):
+        low, high = carry
         lo = pf[0, pl.ds(line, k, stride=lines), :]
         hi = pf[1, pl.ds(line, k, stride=lines), :]
         pt[line // nx, lax.rem(line, nx)] = jnp.concatenate([lo, hi], axis=1).astype(BF16)
-        return lo, hi
-
-    place = lax.broadcasted_iota(jnp.int32, (k, LANES), 1) // 2
-
-    def edge_of(line, carry):
-        low, high = carry
-        lo, hi = turn(line)
         low = jnp.where(place == line, pltpu.roll(lo, 2 * line, 1), low)
         high = jnp.where(place == line, pltpu.roll(hi, lax.rem(2 * line + 2, LANES), 1), high)
         return low, high
 
-    def outer(i, carry):
-        part = lax.rem(i, 4)
-        return edge_of((i // 4) * nx + jnp.where(part < 2, part, nx - 4 + part), carry)
-
-    def inner(i, carry):
-        return edge_of((i // (nx - 4)) * nx + 2 + lax.rem(i, nx - 4), carry)
-
     zero = jnp.zeros((k, LANES), F32)
-    carry = lax.fori_loop(0, nz * 4, outer, (zero, zero))
+    low, high = lax.fori_loop(0, lines, turn, (zero, zero), unroll=4)
+    hs[0] = low.astype(BF16)
+    hs[1] = high.astype(BF16)
+
     pl.semaphore_wait(barrier, count)
-    copies = [
-        remote(pt.at[:, nx - 2 : nx], xh.at[0], send_sem.at[0], recv_sem.at[0], (east, gy)),
-        remote(pt.at[:, 0:2], xh.at[1], send_sem.at[1], recv_sem.at[1], (west, gy)),
+    field_copies = [
         remote(cxs.at[1], cx.at[0], send_sem.at[2], recv_sem.at[2], (east, gy)),
         remote(cxs.at[0], cx.at[1], send_sem.at[3], recv_sem.at[3], (west, gy)),
     ]
-    low, high = lax.fori_loop(0, nz * (nx - 4), inner, carry)
-    hs[0] = low.astype(BF16)
-    hs[1] = high.astype(BF16)
+    probe_copies = []
     used = 4
-    for side, column in ((0, north), (1, south)):
-        for which, row in ((2, west), (1, gx), (0, east)):
-            slot = side * 3 + which
-            source = 1 - side
-            copies.append(
-                remote(hs.at[source], hy.at[slot], send_sem.at[used], recv_sem.at[used], (row, column))
+    arrivals = [
+        (side, which, row, column)
+        for side, column in ((0, north), (1, south))
+        for which, row in ((2, west), (1, gx), (0, east))
+    ]
+    for i, (side, which, row, column) in enumerate(arrivals):
+        slot = side * 3 + which
+        field_copies.append(
+            remote(
+                cys.at[1 - side], cy.at[slot], send_sem.at[4 + i], recv_sem.at[4 + i], (row, column)
             )
-            copies.append(
-                remote(
-                    cys.at[source], cy.at[slot], send_sem.at[used + 1], recv_sem.at[used + 1], (row, column)
-                )
+        )
+    for i, (side, which, row, column) in enumerate(arrivals):
+        slot = side * 3 + which
+        probe_copies.append(
+            remote(
+                hs.at[1 - side], hy.at[slot], send_sem.at[10 + i], recv_sem.at[10 + i], (row, column)
             )
-            used += 2
-    for copy in copies:
-        copy.wait()
-
-
-def sketch_kernel(
-    ng, ny, k, nz, nx, levels, leaf,
-    pt, xh, hy, cx, cy, cond, weights, block, left, right, ranks,
-    shl, gram, leafpart, uc,
-    ce, dg, dd, wd, fx, fyp, fym, fz, f1, a1, wt, acc, cuf,
-):
-    gx, gy = lax.axis_index("gx"), lax.axis_index("gy")
+        )
+    probe_copies += [
+        remote(pt.at[:, nx - 2 : nx], xh.at[0], send_sem.at[0], recv_sem.at[0], (east, gy)),
+        remote(pt.at[:, 0:2], xh.at[1], send_sem.at[1], recv_sem.at[1], (west, gy)),
+    ]
+
     has_west = (gx > 0).astype(F32)
     has_east = (gx < ng - 1).astype(F32)
     has_south = (gy > 0).astype(F32)
@@ -151,6 +185,8 @@
     has_x = (has_west, 1.0, has_east)
     has_y = (has_south, has_north)
     rank = left.shape[1]
+    for load in loads[4:]:
+        load.wait()
 
     wt[0:leaf, :] = block[...].astype(BF16)
     row = lax.broadcasted_iota(jnp.int32, (rank, leaf), 0)
@@ -159,6 +195,9 @@
         at = leaf + 2 * level * rank
         wt[at : at + rank, :] = (right[level] * gain).astype(BF16)
         wt[at + rank : at + 2 * rank, :] = left[level].astype(BF16)
+
+    for copy in field_copies:
+        copy.wait_recv()
 
     tall = nx + 16
     wide = 3 * LANES
@@ -227,21 +266,35 @@
         value = jnp.where(tile_lane < 2, above, 0.0)
         return jnp.where(tile_lane >= LANES - 2, below, value)
 
-    def forward(z, x, value, edge):
+    def inner_tiles(z, x, value):
         inverse = tiles(dd, z, x)
-        parts = split(value) + [edge]
-        store(f1, z, x + 2, [parts[i] * inverse[i] for i in range(3)])
+        parts = split(value)
+        store(f1, z, x + 2, [parts[i] * inverse[i] for i in range(2)])
+
+    def edge_tiles(z, x, edge):
+        f1[z, x + 2, :, 2 * LANES :] = edge * tiles(dd, z, x)[2]
 
     def forward_inner(x, carry):
         for z in range(nz):
-            forward(z, x, pt[z, x].astype(F32), edge_tile(z, x, 1))
+            inner_tiles(z, x, pt[z, x].astype(F32))
         return carry
 
     lax.fori_loop(0, nx, forward_inner, 0)
+    for copy in probe_copies:
+        copy.wait_recv()
+
+    def forward_edges(x, carry):
+        for z in range(nz):
+            edge_tiles(z, x, edge_tile(z, x, 1))
+        return carry
+
+    lax.fori_loop(0, nx, forward_edges, 0)
     for z in range(nz):
         for i in range(2):
-            forward(z, i - 2, xh[0, z, i].astype(F32) * has_west, edge_tile(z, nx - 2 + i, 0))
-            forward(z, nx + i, xh[1, z, i].astype(F32) * has_east, edge_tile(z, i, 2))
+            inner_tiles(z, i - 2, xh[0, z, i].astype(F32) * has_west)
+            edge_tiles(z, i - 2, edge_tile(z, nx - 2 + i, 0))
+            inner_tiles(z, nx + i, xh[1, z, i].astype(F32) * has_east)
+            edge_tiles(z, nx + i, edge_tile(z, i, 2))
 
     def near(ref, z, x, row, count):
         centre = split(ref[z, row])
@@ -318,12 +371,52 @@
 
     lax.fori_loop(0, nx, finish, 0)
 
+    half_k, half_lanes = k // 2, LANES // 2
+    half_lane = lax.broadcasted_iota(jnp.int32, (half_k, LANES), 1)
     pad = jnp.zeros((k, LANES - k), F32)
+
+    def fold(value):
+        value = jnp.concatenate([value, pad], axis=1)
+        return value[:half_k] + pltpu.roll(value[half_k:], half_lanes, 1)
+
+    def unfold(value):
+        first = jnp.where(half_lane < half_lanes, value, 0.0)
+        second = pltpu.roll(jnp.where(half_lane < half_lanes, 0.0, value), half_lanes, 1)
+        return jnp.concatenate([first, second], axis=0) * (1.0 / cells)
+
+    pending = []
+
+    def send(which, stage, value):
+        peers, me = stages[stage]
+        packed[which, stage] = value
+        gathered[which, stage, me] = value
+        copies = [
+            remote(
+                packed.at[which, stage], gathered.at[which, stage, me],
+                sum_send.at[which, stage, d], sum_recv.at[which, stage, d], peer,
+            )
+            for d, peer in enumerate(peers)
+        ]
+        pending.extend(copies)
+        return copies
+
+    def receive(which, stage, copies):
+        for copy in copies:
+            copy.wait_recv()
+        parts = [gathered[which, stage, i] for i in range(len(copies) + 1)]
+        while len(parts) > 1:
+            parts = [
+                parts[i] + parts[i + 1] if i + 1 < len(parts) else parts[i]
+                for i in range(0, len(parts), 2)
+            ]
+        return parts[0]
+
+    store = pltpu.make_async_copy(shl, shl_out, store_sem.at[0])
+    store.start()
     value = acc[...]
     total = value[0:k, 0:k] + (value[0:k, k : 2 * k] + value[k : 2 * k, 0:k]) + value[k:, k : 2 * k]
-    gram[...] = jnp.concatenate([total, pad], axis=1)
-    total = value[0:k, 2 * k :] + value[k:, 2 * k :]
-    leafpart[...] = jnp.concatenate([total, pad], axis=1)
+    first = send(0, 0, fold(total))
+    leafpart = value[0:k, 2 * k :] + value[k:, 2 * k :]
 
     count = LANES // rank
     slot = tile_lane // rank
@@ -344,76 +437,6 @@
         return carry
 
     lax.fori_loop(0, nz * nx // count, gather, 0)
-
-
-def reduce_kernel(
-    ng, ny, k, levels, groups, cells,
-    gram, leafpart, uc,
-    linv, projected,
-    pieces, rs, sums, ar, totals, ag, trees, sems,
-):
-    gx, gy = lax.axis_index("gx"), lax.axis_index("gy")
-    rows = k // ny
-    column = [lax.rem(gy + d, ny) for d in range(1, ny)]
-    across = [lax.rem(gx + d, ng) for d in range(1, ng)]
-    barrier, count = signal_all([(gx, e) for e in column] + [(e, gy) for e in across])
-    send_sem, recv_sem, tree_send, tree_recv = sems
-
-    def scatter(which, value):
-        for i in range(k):
-            pieces[which, i // rows, i % rows, :] = value[i, :]
-        rs[which, gy] = pieces[which, gy]
-        return [
-            remote(
-                pieces.at[which, e], rs.at[which, gy],
-                send_sem.at[which, 0, d], recv_sem.at[which, 0, d], (gx, e),
-            )
-            for d, e in enumerate(column)
-        ]
-
-    def added(ref, which, count):
-        parts = [ref[which, i] for i in range(count)]
-        while len(parts) > 1:
-            parts = [
-                parts[i] + parts[i + 1] if i + 1 < len(parts) else parts[i]
-                for i in range(0, len(parts), 2)
-            ]
-        return parts[0]
-
-    def exchange(which, copies):
-        for copy in copies:
-            copy.wait()
-        sums[which] = added(rs, which, ny)
-        ar[which, gx] = sums[which]
-        return [
-            remote(
-                sums.at[which], ar.at[which, gx],
-                send_sem.at[which, 1, d], recv_sem.at[which, 1, d], (e, gy),
-            )
-            for d, e in enumerate(across)
-        ]
-
-    def spread(which, copies):
-        for copy in copies:
-            copy.wait()
-        totals[which] = added(ar, which, ng)
-        ag[which, gy] = totals[which]
-        return [
-            remote(
-                totals.at[which], ag.at[which, gy],
-                send_sem.at[which, 2, d], recv_sem.at[which, 2, d], (gx, e),
-            )
-            for d, e in enumerate(column)
-        ]
-
-    def collect(which, copies):
-        for copy in copies:
-            copy.wait()
-        parts = [ag[which, i // rows, i % rows : i % rows + 1, :] for i in range(k)]
-        return jnp.concatenate(parts, axis=0) * (1.0 / cells)
-
-    pl.semaphore_wait(barrier, count)
-    flight = scatter(0, gram[...])
 
     def flipped(bits):
         device = gy
@@ -438,10 +461,10 @@
                 )
             )
 
-    flight = exchange(0, flight)
+    first = send(0, 1, receive(0, 0, first))
     for copy in tree:
-        copy.wait()
-    total = leafpart[:, 0:k]
+        copy.wait_recv()
+    total = leafpart
     for level in range(levels):
         half = 2**level
         share = groups // half
@@ -456,10 +479,10 @@
             total = total + lax.dot_general(
                 own.astype(BF16), other.astype(BF16), NT, preferred_element_type=F32
             )
-    total = jnp.concatenate([total, jnp.zeros((k, LANES - k), F32)], axis=1)
-    flight = spread(0, flight)
-    second = scatter(1, total)
-    matrix = collect(0, flight)
+    second = send(1, 0, fold(total))
+    first = send(0, 2, receive(0, 1, first))
+    second = send(1, 1, receive(1, 0, second))
+    matrix = unfold(receive(0, 2, first))
 
     row = lax.broadcasted_iota(jnp.int32, (k, LANES), 0)
     lane = lax.broadcasted_iota(jnp.int32, (k, LANES), 1)
@@ -477,22 +500,30 @@
             if i == t:
                 change = jnp.where(inner > s, change, 0.0)
             blocks[i] = blocks[i] - change
-        if j == k // 3:
-            second = exchange(1, second)
-        if j == k - k // 6:
-            second = spread(1, second)
+        if j == k // 4:
+            second = send(1, 2, receive(1, 1, second))
     whole = jnp.concatenate(blocks, axis=0)
     pivots = jnp.sum(jnp.where(lane == row, whole, 0.0), axis=1, keepdims=True)
     inverse = whole[:, start : start + k] / jnp.sqrt(pivots)
-    linv[...] = inverse
-    middle = collect(1, second)[:, 0:k]
-    product = jnp.dot(inverse, middle, precision=HIGH, preferred_element_type=F32)
-    product = lax.dot_general(product, inverse, NT, precision=HIGH, preferred_element_type=F32)
-    projected[...] = product + jnp.where(lane[:, 0:k] == row[:, 0:k], 1.0, 0.0)
-
-
-def basis_kernel(k, nz, nx, shl, linv, out, buffer, sem):
-    inverse = linv[...]
+    small[0] = inverse
+    small[1] = unfold(receive(1, 2, second))[:, 0:k]
+    last = pltpu.make_async_copy(small, small_out, store_sem.at[1])
+    last.start()
+    for copy in field_copies + probe_copies + tree + pending:
+        copy.wait_send()
+    store.wait()
+    last.wait()
+
+
+def basis_kernel(k, nz, nx, shl_in, small_in, out, projected, shl, small, buffer, load_sem, sem):
+    loads = [pltpu.make_async_copy(small_in, small, load_sem.at[nz])]
+    for z in range(nz):
+        lines = pl.ds(z * nx, nx)
+        loads.append(pltpu.make_async_copy(shl_in.at[lines], shl.at[lines], load_sem.at[z]))
+    for load in loads:
+        load.start()
+    loads[0].wait()
+    inverse = small[0]
     high = inverse.astype(BF16)
     low = (inverse - high.astype(F32)).astype(BF16)
     lhs = jnp.concatenate(
@@ -504,6 +535,7 @@
     )
     copies = []
     for z in range(nz):
+        loads[z + 1].wait()
 
         def one(x, carry):
             value = jnp.dot(lhs, shl[z * nx + x], preferred_element_type=F32)
@@ -521,12 +553,17 @@
             )
             copy.start()
             copies.append(copy)
+    product = jnp.dot(inverse, small[1], precision=HIGH, preferred_element_type=F32)
+    product = lax.dot_general(product, inverse, NT, precision=HIGH, preferred_element_type=F32)
+    row = lax.broadcasted_iota(jnp.int32, (k, k), 0)
+    lane = lax.broadcasted_iota(jnp.int32, (k, k), 1)
+    projected[...] = product + jnp.where(lane == row, 1.0, 0.0)
     for copy in copies:
         copy.wait()
 
 
 def params(**more):
-    return pltpu.CompilerParams(vmem_limit_bytes=40 * 2**20, **more)
+    return pltpu.CompilerParams(vmem_limit_bytes=56 * 2**20, **more)
 
 
 def shards(
@@ -541,94 +578,88 @@
     cells = float(nz * nx * leaf * ng * ny)
     shape = jax.ShapeDtypeStruct
     dma = pltpu.SemaphoreType.DMA
-
-    pt, xh, hy, cx, cy, cond = pl.pallas_call(
-        functools.partial(halo_kernel, ng, ny, k, nz, nx),
+    vmem = pltpu.VMEM
+    edges = 2 * ny
+    most = 8
+    while most < max(ng // min(4, ng), ny // min(2, ny)):
+        most *= 2
+
+    field = vmem((nz, nx + 16, 3 * LANES), F32)
+    shl, small = pl.pallas_call(
+        functools.partial(
+            sketch_kernel, ng, ny, k, nz, nx, levels, leaf, groups, cells
+        ),
         out_shape=(
-            shape((nz, nx, k, leaf), BF16),
-            shape((2, nz, 2, k, leaf), BF16),
-            shape((6, k, LANES), BF16),
-            shape((2, 4 * nz, leaf), F32),
-            shape((6, nx, LANES), F32),
-            shape((nz, nx, leaf), F32),
+            shape((lines, 2 * k, leaf), BF16),
+            shape((2, k, k), F32),
         ),
-        in_specs=[VMEM, VMEM, SMEM, VMEM],
-        out_specs=(VMEM,) * 6,
+        in_specs=[HBM] * 8,
+        out_specs=(HBM,) * 2,
         scratch_shapes=[
-            pltpu.VMEM((2, k * lines, LANES), F32),
-            pltpu.VMEM((2, k, LANES), BF16),
-            pltpu.VMEM((2, 4 * nz, leaf), F32),
-            pltpu.VMEM((2, nx, LANES), F32),
+            vmem((lines, 2 * k, leaf), BF16),
+            vmem((2, k, k), F32),
+            dma((2,)),
+            vmem((k * lines, leaf), BF16),
+            vmem(classes.shape, classes.dtype),
+            pltpu.SMEM(class_table.shape, F32),
+            vmem(weights.shape, F32),
+            vmem(prior_block.shape, F32),
+            vmem((levels, rank, leaf), F32),
+            vmem((levels, rank, leaf), F32),
+            pltpu.SMEM(block_ranks.shape, block_ranks.dtype),
+            dma((8,)),
+            vmem((nz, nx, k, leaf), BF16),
+            vmem((nz, nx, leaf), F32),
+            vmem((2, k * lines, LANES), F32),
+            vmem((2, nz, 2, k, leaf), BF16),
+            vmem((6, k, LANES), BF16),
+            vmem((2, 4 * nz, leaf), F32),
+            vmem((6, nx, LANES), F32),
+            vmem((2, k, LANES), BF16),
+            vmem((2, 4 * nz, leaf), F32),
+            vmem((2, nx, LANES), F32),
             dma((16,)),
             dma((16,)),
+        ]
+        + [field] * 8
+        + [
+            vmem((nz, nx + 4, k, 3 * LANES), F32),
+            vmem((nz, nx + 2, k, 3 * LANES), F32),
+            vmem((leaf + LANES, leaf), BF16),
+            vmem((2 * k, 3 * k), F32),
+            vmem((lines, k, LANES), F32),
+            vmem((2 * levels, groups, k, LANES), BF16),
+            [
+                vmem((2 ** (level + 1) - 1, groups >> level, k, LANES), BF16)
+                for level in range(levels)
+            ],
+            dma((edges,)),
+            dma((edges,)),
+            vmem((2, 3, k // 2, LANES), F32),
+            vmem((2, 3, most, k // 2, LANES), F32),
+            dma((2, 3, most)),
+            dma((2, 3, most)),
         ],
         compiler_params=params(collective_id=0, has_side_effects=True),
-    )(probes.reshape(k * lines, leaf), classes, class_table, weights)
-
-    field = pltpu.VMEM((nz, nx + 16, 3 * LANES), F32)
-    shl, gram, leafpart, uc = pl.pallas_call(
-        functools.partial(sketch_kernel, ng, ny, k, nz, nx, levels, leaf),
-        out_shape=(
-            shape((lines, 2 * k, leaf), BF16),
-            shape((k, LANES), F32),
-            shape((k, LANES), F32),
-            shape((2 * levels, groups, k, LANES), BF16),
-        ),
-        in_specs=[VMEM] * 10 + [SMEM],
-        out_specs=(VMEM,) * 4,
-        scratch_shapes=[field] * 8
-        + [
-            pltpu.VMEM((nz, nx + 4, k, 3 * LANES), F32),
-            pltpu.VMEM((nz, nx + 2, k, 3 * LANES), F32),
-            pltpu.VMEM((leaf + LANES, leaf), BF16),
-            pltpu.VMEM((2 * k, 3 * k), F32),
-            pltpu.VMEM((lines, k, LANES), F32),
-        ],
-        compiler_params=params(),
     )(
-        pt, xh, hy, cx, cy, cond, weights, prior_block, prior_left[:levels],
-        prior_right[:levels], block_ranks,
+        probes.reshape(k * lines, leaf), classes, class_table, weights, prior_block, prior_left,
+        prior_right, block_ranks,
     )
 
-    rows = k // ny
-    edges = 2 * ny
-    linv, projected = pl.pallas_call(
-        functools.partial(reduce_kernel, ng, ny, k, levels, groups, cells),
-        out_shape=(shape((k, k), F32), shape((k, k), F32)),
-        in_specs=[VMEM] * 3,
-        out_specs=(VMEM, VMEM),
+    basis, projected = pl.pallas_call(
+        functools.partial(basis_kernel, k, nz, nx),
+        out_shape=(shape((k, nz, nx, leaf), F32), shape((k, k), F32)),
+        in_specs=[HBM] * 2,
+        out_specs=(HBM, VMEM),
         scratch_shapes=[
-            pltpu.VMEM((2, ny, rows, LANES), F32),
-            pltpu.VMEM((2, ny, rows, LANES), F32),
-            pltpu.VMEM((2, rows, LANES), F32),
-            pltpu.VMEM((2, ng, rows, LANES), F32),
-            pltpu.VMEM((2, rows, LANES), F32),
-            pltpu.VMEM((2, ny, rows, LANES), F32),
-            [
-                pltpu.VMEM((2 ** (level + 1) - 1, groups >> level, k, LANES), BF16)
-                for level in range(levels)
-            ],
-            [
-                dma((2, 3, max(ny, ng))),
-                dma((2, 3, max(ny, ng))),
-                dma((edges,)),
-                dma((edges,)),
-            ],
-        ],
-        compiler_params=params(collective_id=1, has_side_effects=True),
-    )(gram, leafpart, uc)
-
-    basis = pl.pallas_call(
-        functools.partial(basis_kernel, k, nz, nx),
-        out_shape=shape((k, nz, nx, leaf), F32),
-        in_specs=[VMEM, VMEM],
-        out_specs=ANY,
-        scratch_shapes=[
-            pltpu.VMEM((nz, 2, k * nx, LANES), F32),
+            vmem((lines, 2 * k, leaf), BF16),
+            vmem((2, k, k), F32),
+            vmem((nz, 2, k * nx, LANES), F32),
+            dma((nz + 1,)),
             dma((nz, 2)),
         ],
         compiler_params=params(),
-    )(shl, linv)
+    )(shl, small)
     return basis, projected
 
 

time: 101 us -> 81.5 us (0.81)
  Pallas kernels: 92.1 us -> 80.8 us
  local copies, waits for them, and re-layouts: 7.64 us -> 0 us
    pallas_call x3 -> x1, Pallas kernels: 74 us -> 6.26 us  [shards(): pl.pallas_call(functools.partial(basis_kernel, k, nz, nx), out_shape=(sha...]
    pallas_call x1, Pallas kernels: 18.1 us -> 74.5 us  [shards(): pl.pallas_call(functools.partial(sketch_kernel, ng, ny, k, nz, nx, levels...]
    unnamed x13 -> x0, local copies, waits for them, and re-layouts: 5.95 us -> none
    slice x2 -> x0, local copies, waits for them, and re-layouts: 1.69 us -> none  [the longest x1 0.85 us: shards(): prior_left[:levels]]
where the time goes in v1:
time: 81.5 us; the launch traced here: 81.4 us
  Pallas kernels  80.8 us (99%)
    pallas_call x1, Pallas kernels, shards(): pl.pallas_call(functools.partial(sketch_kernel, ng, ny, k, nz, nx, levels...  74.5 us
    pallas_call x1, Pallas kernels, shards(): pl.pallas_call(functools.partial(basis_kernel, k, nz, nx), out_shape=(sha...  6.26 us

profile of v1, /device:TPU:1, one launch (start us, length us, event | category | flops | bytes accessed | tf_op | source)
XLA Modules:
  0.0 81.4 jit_solution(17012923664079990553)
XLA Ops:
  0.6 74.5 %shard_map.95 = (bf16[64,96,256]{2,1,0:T(8,128)(2,1)}, f32[2,48,48]{2,1,0:T(8,128)}) custom-call(bf16[3072,256]{1,0:T(8,128)(2,1)} %bitcast.1, s32[4,16,256]{2,1,0:T(8,128)} %classes_in.1, f32[8]{0:T(128)} %table_in.1, f32[4,16,256]{2,1,0:T(8,128)} %weights_in.1, f32[256,256]{1,0:T(8,128)} %block_in.1, f32[8,16,256]{2,1,0:T(8,128)} %left_in.1, ...), custom_call_target="tpu_custom_call" | custom-call | tf_op jit(solution)/shard_map/pallas_call | solution.py:588
  75.1 6.3 %shard_map.96 = (f32[48,4,16,256]{3,2,1,0:T(8,128)}, f32[48,48]{1,0:T(8,128)}) custom-call(bf16[64,96,256]{2,1,0:T(8,128)(2,1)} %get-tuple-element.4.shl_in, f32[2,48,48]{2,1,0:T(8,128)} %get-tuple-element.5.small_in), custom_call_target="tpu_custom_call" | custom-call | tf_op jit(solution)/shard_map/pallas_call | solution.py:649

commit v2 on v1

--- a/solution.py
+++ b/solution.py
@@ -37,8 +37,8 @@
 def sketch_kernel(
     ng, ny, k, nz, nx, levels, leaf, groups, cells,
     probes_in, classes_in, table_in, weights_in, block_in, left_in, right_in, ranks_in,
-    shl_out, small_out,
-    shl, small, store_sem, probes, classes, table, weights, block, left, right, ranks, load_sem,
+    out, projected,
+    shl, buffer, store_sem, probes, classes, table, weights, block, left, right, ranks, load_sem,
     pt, cond, pf, xh, hy, cx, cy, hs, cxs, cys, send_sem, recv_sem,
     ce, dg, dd, wd, fx, fyp, fym, fz, f1, a1, wt, acc, cuf, uc,
     trees, tree_send, tree_recv, packed, gathered, sum_send, sum_recv,
@@ -66,11 +66,11 @@
             ],
             at_c * across + at_x,
         ),
+        ([(lax.rem(at_z + d, deep) * across + at_x, gy) for d in range(1, deep)], at_z),
         ([(gx, lax.rem(at_y + d, high_y) * pair + at_c) for d in range(1, high_y)], at_y),
-        ([(lax.rem(at_z + d, deep) * across + at_x, gy) for d in range(1, deep)], at_z),
     ]
     column = [(gx, lax.rem(gy + d, ny)) for d in range(1, ny)]
-    barrier, count = signal_all(around + stages[0][0] + stages[2][0] + column)
+    barrier, count = signal_all(around + stages[0][0] + stages[1][0] + column)
 
     loads = [
         pltpu.make_async_copy(source, target, load_sem.at[i])
@@ -280,7 +280,7 @@
         return carry
 
     lax.fori_loop(0, nx, forward_inner, 0)
-    for copy in probe_copies:
+    for copy in probe_copies[:6]:
         copy.wait_recv()
 
     def forward_edges(x, carry):
@@ -289,13 +289,6 @@
         return carry
 
     lax.fori_loop(0, nx, forward_edges, 0)
-    for z in range(nz):
-        for i in range(2):
-            inner_tiles(z, i - 2, xh[0, z, i].astype(F32) * has_west)
-            edge_tiles(z, i - 2, edge_tile(z, nx - 2 + i, 0))
-            inner_tiles(z, nx + i, xh[1, z, i].astype(F32) * has_east)
-            edge_tiles(z, nx + i, edge_tile(z, i, 2))
-
     def near(ref, z, x, row, count):
         centre = split(ref[z, row])
         ahead = [pltpu.roll(part, LANES - 1, 1) for part in centre]
@@ -330,8 +323,6 @@
             ]
             store(a1, z, x + 1, parts)
         return carry
-
-    lax.fori_loop(0, nx + 2, adjoint, 0)
 
     acc[...] = jnp.zeros_like(acc)
 
@@ -369,7 +360,25 @@
         acc[...] += lax.dot_general(lhs, rhs, NT, preferred_element_type=F32)
         return carry
 
-    lax.fori_loop(0, nx, finish, 0)
+    lax.fori_loop(2, nx, adjoint, 0)
+    lax.fori_loop(2, nx - 2, finish, 0)
+    for copy in probe_copies[6:]:
+        copy.wait_recv()
+    for z in range(nz):
+        for i in range(2):
+            inner_tiles(z, i - 2, xh[0, z, i].astype(F32) * has_west)
+            edge_tiles(z, i - 2, edge_tile(z, nx - 2 + i, 0))
+            inner_tiles(z, nx + i, xh[1, z, i].astype(F32) * has_east)
+            edge_tiles(z, nx + i, edge_tile(z, i, 2))
+
+    def adjoint_outer(i, carry):
+        return adjoint(jnp.where(i < 2, i, nx - 2 + i), carry)
+
+    def finish_outer(i, carry):
+        return finish(jnp.where(i < 2, i, nx - 4 + i), carry)
+
+    lax.fori_loop(0, 4, adjoint_outer, 0)
+    lax.fori_loop(0, 4, finish_outer, 0)
 
     half_k, half_lanes = k // 2, LANES // 2
     half_lane = lax.broadcasted_iota(jnp.int32, (half_k, LANES), 1)
@@ -411,8 +420,6 @@
             ]
         return parts[0]
 
-    store = pltpu.make_async_copy(shl, shl_out, store_sem.at[0])
-    store.start()
     value = acc[...]
     total = value[0:k, 0:k] + (value[0:k, k : 2 * k] + value[k : 2 * k, 0:k]) + value[k:, k : 2 * k]
     first = send(0, 0, fold(total))
@@ -462,6 +469,7 @@
             )
 
     first = send(0, 1, receive(0, 0, first))
+    first = send(0, 2, receive(0, 1, first))
     for copy in tree:
         copy.wait_recv()
     total = leafpart
@@ -480,8 +488,6 @@
                 own.astype(BF16), other.astype(BF16), NT, preferred_element_type=F32
             )
     second = send(1, 0, fold(total))
-    first = send(0, 2, receive(0, 1, first))
-    second = send(1, 1, receive(1, 0, second))
     matrix = unfold(receive(0, 2, first))
 
     row = lax.broadcasted_iota(jnp.int32, (k, LANES), 0)
@@ -500,30 +506,12 @@
             if i == t:
                 change = jnp.where(inner > s, change, 0.0)
             blocks[i] = blocks[i] - change
-        if j == k // 4:
-            second = send(1, 2, receive(1, 1, second))
+        if j == k // 2:
+            second = send(1, 1, receive(1, 0, second))
     whole = jnp.concatenate(blocks, axis=0)
     pivots = jnp.sum(jnp.where(lane == row, whole, 0.0), axis=1, keepdims=True)
     inverse = whole[:, start : start + k] / jnp.sqrt(pivots)
-    small[0] = inverse
-    small[1] = unfold(receive(1, 2, second))[:, 0:k]
-    last = pltpu.make_async_copy(small, small_out, store_sem.at[1])
-    last.start()
-    for copy in field_copies + probe_copies + tree + pending:
-        copy.wait_send()
-    store.wait()
-    last.wait()
-
-
-def basis_kernel(k, nz, nx, shl_in, small_in, out, projected, shl, small, buffer, load_sem, sem):
-    loads = [pltpu.make_async_copy(small_in, small, load_sem.at[nz])]
-    for z in range(nz):
-        lines = pl.ds(z * nx, nx)
-        loads.append(pltpu.make_async_copy(shl_in.at[lines], shl.at[lines], load_sem.at[z]))
-    for load in loads:
-        load.start()
-    loads[0].wait()
-    inverse = small[0]
+
     high = inverse.astype(BF16)
     low = (inverse - high.astype(F32)).astype(BF16)
     lhs = jnp.concatenate(
@@ -533,9 +521,8 @@
         ],
         axis=0,
     )
-    copies = []
+    stores = []
     for z in range(nz):
-        loads[z + 1].wait()
 
         def one(x, carry):
             value = jnp.dot(lhs, shl[z * nx + x], preferred_element_type=F32)
@@ -549,16 +536,19 @@
             copy = pltpu.make_async_copy(
                 buffer.at[z, i].reshape(k, nx, LANES),
                 out.at[:, z, :, i * LANES : (i + 1) * LANES],
-                sem.at[z, i],
+                store_sem.at[z, i],
             )
             copy.start()
-            copies.append(copy)
-    product = jnp.dot(inverse, small[1], precision=HIGH, preferred_element_type=F32)
+            stores.append(copy)
+        if z == nz // 2:
+            second = send(1, 2, receive(1, 1, second))
+    middle = unfold(receive(1, 2, second))[:, 0:k]
+    product = jnp.dot(inverse, middle, precision=HIGH, preferred_element_type=F32)
     product = lax.dot_general(product, inverse, NT, precision=HIGH, preferred_element_type=F32)
-    row = lax.broadcasted_iota(jnp.int32, (k, k), 0)
-    lane = lax.broadcasted_iota(jnp.int32, (k, k), 1)
-    projected[...] = product + jnp.where(lane == row, 1.0, 0.0)
-    for copy in copies:
+    projected[...] = product + jnp.where(lane[:, 0:k] == row[:, 0:k], 1.0, 0.0)
+    for copy in field_copies + probe_copies + tree + pending:
+        copy.wait_send()
+    for copy in stores:
         copy.wait()
 
 
@@ -585,20 +575,20 @@
         most *= 2
 
     field = vmem((nz, nx + 16, 3 * LANES), F32)
-    shl, small = pl.pallas_call(
+    basis, projected = pl.pallas_call(
         functools.partial(
             sketch_kernel, ng, ny, k, nz, nx, levels, leaf, groups, cells
         ),
         out_shape=(
-            shape((lines, 2 * k, leaf), BF16),
-            shape((2, k, k), F32),
+            shape((k, nz, nx, leaf), F32),
+            shape((k, k), F32),
         ),
         in_specs=[HBM] * 8,
-        out_specs=(HBM,) * 2,
+        out_specs=(HBM, VMEM),
         scratch_shapes=[
             vmem((lines, 2 * k, leaf), BF16),
-            vmem((2, k, k), F32),
-            dma((2,)),
+            vmem((nz, 2, k * nx, LANES), F32),
+            dma((nz, 2)),
             vmem((k * lines, leaf), BF16),
             vmem(classes.shape, classes.dtype),
             pltpu.SMEM(class_table.shape, F32),
@@ -645,21 +635,6 @@
         probes.reshape(k * lines, leaf), classes, class_table, weights, prior_block, prior_left,
         prior_right, block_ranks,
     )
-
-    basis, projected = pl.pallas_call(
-        functools.partial(basis_kernel, k, nz, nx),
-        out_shape=(shape((k, nz, nx, leaf), F32), shape((k, k), F32)),
-        in_specs=[HBM] * 2,
-        out_specs=(HBM, VMEM),
-        scratch_shapes=[
-            vmem((lines, 2 * k, leaf), BF16),
-            vmem((2, k, k), F32),
-            vmem((nz, 2, k * nx, LANES), F32),
-            dma((nz + 1,)),
-            dma((nz, 2)),
-        ],
-        compiler_params=params(),
-    )(shl, small)
     return basis, projected
 
 

time: 81.5 us -> 75.4 us (0.925)
  Pallas kernels: 80.8 us -> 69.9 us
  local copies, waits for them, and re-layouts: 0 us -> 4.72 us
    pallas_call x1 -> x0, Pallas kernels: 6.26 us -> none  [shards(): pl.pallas_call(functools.partial(basis_kernel, k, nz, nx), out_shape=(sha...]
    unnamed x0 -> x4, local copies, waits for them, and re-layouts: none -> 4.72 us
    pallas_call x1, Pallas kernels: 74.5 us -> 69.9 us  [shards(): pl.pallas_call(functools.partial(sketch_kernel, ng, ny, k, nz, nx, levels...]
where the time goes in v2:
time: 75.4 us; the launch traced here: 75.3 us
  Pallas kernels  69.9 us (93%)
  local copies, waits for them, and re-layouts  4.72 us (6%)
    pallas_call x1, Pallas kernels, shards(): pl.pallas_call(functools.partial(sketch_kernel, ng, ny, k, nz, nx, levels...  69.9 us
    unnamed x4, local copies, waits for them, and re-layouts  4.72 us

profile of v2, /device:TPU:1, one launch (start us, length us, event | category | flops | bytes accessed | tf_op | source)
XLA Modules:
  0.0 75.3 jit_solution(10566463460864097341)
XLA Ops:
  0.6 69.9 %shard_map.95 = (f32[48,4,16,256]{3,2,1,0:T(8,128)}, f32[48,48]{1,0:T(8,128)}) custom-call(bf16[3072,256]{1,0:T(8,128)(2,1)} %bitcast.1, s32[4,16,256]{2,1,0:T(8,128)} %classes_in.1, f32[8]{0:T(128)} %table_in.1, f32[4,16,256]{2,1,0:T(8,128)} %weights_in.1, f32[256,256]{1,0:T(8,128)} %block_in.1, f32[8,16,256]{2,1,0:T(8,128)} %left_in.1, ...), custom_call_target="tpu_custom_call" | custom-call | tf_op jit(solution)/shard_map/pallas_call | solution.py:578
  70.5 0.0 copy-start
  70.6 4.1 %copy.12 = f32[48,4,16,256]{3,2,1,0:T(8,128)} copy(f32[48,4,16,256]{3,2,1,0:T(8,128)} %get-tuple-element.4) | data formatting | bytes 6291456
  74.7 0.0 copy-done
  74.7 0.6 copy.13
Async XLA Ops:
  70.5 4.1 %copy-start = (f32[48,48]{1,0:T(8,128)S(1)}, f32[48,48]{1,0:T(8,128)}, u32[]{:S(2)}) copy-start(f32[48,48]{1,0:T(8,128)} %get-tuple-element.5) | copy-start | bytes 27652

commit v3 on v2

--- a/solution.py
+++ b/solution.py
@@ -326,7 +326,7 @@
 
     acc[...] = jnp.zeros_like(acc)
 
-    def finish(x, carry):
+    def finish(x, slot, apart):
         whole_high, whole_low = [], []
         for z in range(nz):
             centre, sums = near(a1, z, x, x + 1, 2)
@@ -351,79 +351,23 @@
         rows = []
         for z in range(nz):
             part = applied[z * k : (z + 1) * k]
-            cuf[z * nx + x] = part[:, leaf:]
+            cuf[slot + z * apart] = part[:, leaf:]
             rows.append(part[:, :leaf].astype(BF16))
         high = jnp.concatenate(whole_high, axis=1)
         low = jnp.concatenate(whole_low, axis=1)
         lhs = jnp.concatenate([high, low], axis=0)
         rhs = jnp.concatenate([high, low, jnp.concatenate(rows, axis=1)], axis=0)
         acc[...] += lax.dot_general(lhs, rhs, NT, preferred_element_type=F32)
+
+    lax.fori_loop(2, nx, adjoint, 0)
+    inner_rows = nx - 4
+    early = nz * inner_rows // (LANES // rank)
+
+    def finish_inner(x, carry):
+        finish(x, x - 2, inner_rows)
         return carry
 
-    lax.fori_loop(2, nx, adjoint, 0)
-    lax.fori_loop(2, nx - 2, finish, 0)
-    for copy in probe_copies[6:]:
-        copy.wait_recv()
-    for z in range(nz):
-        for i in range(2):
-            inner_tiles(z, i - 2, xh[0, z, i].astype(F32) * has_west)
-            edge_tiles(z, i - 2, edge_tile(z, nx - 2 + i, 0))
-            inner_tiles(z, nx + i, xh[1, z, i].astype(F32) * has_east)
-            edge_tiles(z, nx + i, edge_tile(z, i, 2))
-
-    def adjoint_outer(i, carry):
-        return adjoint(jnp.where(i < 2, i, nx - 2 + i), carry)
-
-    def finish_outer(i, carry):
-        return finish(jnp.where(i < 2, i, nx - 4 + i), carry)
-
-    lax.fori_loop(0, 4, adjoint_outer, 0)
-    lax.fori_loop(0, 4, finish_outer, 0)
-
-    half_k, half_lanes = k // 2, LANES // 2
-    half_lane = lax.broadcasted_iota(jnp.int32, (half_k, LANES), 1)
-    pad = jnp.zeros((k, LANES - k), F32)
-
-    def fold(value):
-        value = jnp.concatenate([value, pad], axis=1)
-        return value[:half_k] + pltpu.roll(value[half_k:], half_lanes, 1)
-
-    def unfold(value):
-        first = jnp.where(half_lane < half_lanes, value, 0.0)
-        second = pltpu.roll(jnp.where(half_lane < half_lanes, 0.0, value), half_lanes, 1)
-        return jnp.concatenate([first, second], axis=0) * (1.0 / cells)
-
-    pending = []
-
-    def send(which, stage, value):
-        peers, me = stages[stage]
-        packed[which, stage] = value
-        gathered[which, stage, me] = value
-        copies = [
-            remote(
-                packed.at[which, stage], gathered.at[which, stage, me],
-                sum_send.at[which, stage, d], sum_recv.at[which, stage, d], peer,
-            )
-            for d, peer in enumerate(peers)
-        ]
-        pending.extend(copies)
-        return copies
-
-    def receive(which, stage, copies):
-        for copy in copies:
-            copy.wait_recv()
-        parts = [gathered[which, stage, i] for i in range(len(copies) + 1)]
-        while len(parts) > 1:
-            parts = [
-                parts[i] + parts[i + 1] if i + 1 < len(parts) else parts[i]
-                for i in range(0, len(parts), 2)
-            ]
-        return parts[0]
-
-    value = acc[...]
-    total = value[0:k, 0:k] + (value[0:k, k : 2 * k] + value[k : 2 * k, 0:k]) + value[k:, k : 2 * k]
-    first = send(0, 0, fold(total))
-    leafpart = value[0:k, 2 * k :] + value[k:, 2 * k :]
+    lax.fori_loop(2, nx - 2, finish_inner, 0)
 
     count = LANES // rank
     slot = tile_lane // rank
@@ -443,7 +387,7 @@
             uc[index, group] = parts[index].astype(BF16)
         return carry
 
-    lax.fori_loop(0, nz * nx // count, gather, 0)
+    lax.fori_loop(0, early, gather, 0)
 
     def flipped(bits):
         device = gy
@@ -460,19 +404,94 @@
             peer = flipped(bits)
             kind = 2 * level + (1 if bits < half else 0)
             begin = lax.rem(peer, half) * share
-            tree.append(
-                remote(
-                    uc.at[kind, pl.ds(begin, share)], trees[level].at[bits - 1],
-                    tree_send.at[2 * half - 2 - level + bits], tree_recv.at[2 * half - 2 - level + bits],
-                    (gx, peer),
-                )
+            copy = pltpu.make_async_remote_copy(
+                src_ref=uc.at[kind, pl.ds(begin, share)],
+                dst_ref=trees[level].at[bits - 1],
+                send_sem=tree_send.at[2 * half - 2 - level + bits],
+                recv_sem=tree_recv.at[2 * half - 2 - level + bits],
+                device_id=(gx, peer),
+                device_id_type=MESH,
             )
+            tree.append((copy, lax.rem(peer, half) < early // share, early < share))
+
+    for copy, ready, never in tree:
+        if not never:
+            pl.when(ready)(copy.start)
+    for copy in probe_copies[6:]:
+        copy.wait_recv()
+    for z in range(nz):
+        for i in range(2):
+            inner_tiles(z, i - 2, xh[0, z, i].astype(F32) * has_west)
+            edge_tiles(z, i - 2, edge_tile(z, nx - 2 + i, 0))
+            inner_tiles(z, nx + i, xh[1, z, i].astype(F32) * has_east)
+            edge_tiles(z, nx + i, edge_tile(z, i, 2))
+
+    def adjoint_outer(i, carry):
+        return adjoint(jnp.where(i < 2, i, nx - 2 + i), carry)
+
+    def finish_outer(i, carry):
+        finish(jnp.where(i < 2, i, nx - 4 + i), nz * inner_rows + i, 4)
+        return carry
+
+    lax.fori_loop(0, 4, adjoint_outer, 0)
+    lax.fori_loop(0, 4, finish_outer, 0)
+
+    half_k, half_lanes = k // 2, LANES // 2
+    half_lane = lax.broadcasted_iota(jnp.int32, (half_k, LANES), 1)
+    pad = jnp.zeros((k, LANES - k), F32)
+
+    def fold(value):
+        value = jnp.concatenate([value, pad], axis=1)
+        return value[:half_k] + pltpu.roll(value[half_k:], half_lanes, 1)
+
+    def unfold(value):
+        first = jnp.where(half_lane < half_lanes, value, 0.0)
+        second = pltpu.roll(jnp.where(half_lane < half_lanes, 0.0, value), half_lanes, 1)
+        return jnp.concatenate([first, second], axis=0) * (1.0 / cells)
+
+    pending = []
+
+    def send(which, stage, value):
+        peers, me = stages[stage]
+        packed[which, stage] = value
+        gathered[which, stage, me] = value
+        copies = [
+            remote(
+                packed.at[which, stage], gathered.at[which, stage, me],
+                sum_send.at[which, stage, d], sum_recv.at[which, stage, d], peer,
+            )
+            for d, peer in enumerate(peers)
+        ]
+        pending.extend(copies)
+        return copies
+
+    def receive(which, stage, copies):
+        for copy in copies:
+            copy.wait_recv()
+        parts = [gathered[which, stage, i] for i in range(len(copies) + 1)]
+        while len(parts) > 1:
+            parts = [
+                parts[i] + parts[i + 1] if i + 1 < len(parts) else parts[i]
+                for i in range(0, len(parts), 2)
+            ]
+        return parts[0]
+
+    value = acc[...]
+    total = value[0:k, 0:k] + (value[0:k, k : 2 * k] + value[k : 2 * k, 0:k]) + value[k:, k : 2 * k]
+    first = send(0, 0, fold(total))
+    leafpart = value[0:k, 2 * k :] + value[k:, 2 * k :]
+
+    lax.fori_loop(early, groups, gather, 0)
+    for copy, ready, never in tree:
+        if never:
+            copy.start()
+        else:
+            pl.when(jnp.logical_not(ready))(copy.start)
 
     first = send(0, 1, receive(0, 0, first))
-    first = send(0, 2, receive(0, 1, first))
-    for copy in tree:
+    for copy, _, _ in tree:
         copy.wait_recv()
-    total = leafpart
+    lefts, rights = [], []
     for level in range(levels):
         half = 2**level
         share = groups // half
@@ -484,10 +503,17 @@
             other = trees[level][half - 1, j].astype(F32)
             for bits in range(half + 1, 2 * half):
                 other = other + trees[level][bits - 1, j].astype(F32)
-            total = total + lax.dot_general(
-                own.astype(BF16), other.astype(BF16), NT, preferred_element_type=F32
-            )
+            lefts.append(own.astype(BF16))
+            rights.append(other.astype(BF16))
+    total = leafpart + lax.dot_general(
+        jnp.concatenate(lefts, axis=1),
+        jnp.concatenate(rights, axis=1),
+        NT,
+        preferred_element_type=F32,
+    )
     second = send(1, 0, fold(total))
+    first = send(0, 2, receive(0, 1, first))
+    second = send(1, 1, receive(1, 0, second))
     matrix = unfold(receive(0, 2, first))
 
     row = lax.broadcasted_iota(jnp.int32, (k, LANES), 0)
@@ -496,18 +522,27 @@
     whole = jnp.where(lane < k, matrix, jnp.where(lane == row + start, 1.0, 0.0))
     blocks = [whole[8 * t : 8 * t + 8] for t in range(k // 8)]
     inner = lax.broadcasted_iota(jnp.int32, (8, LANES), 0)
-    for j in range(k):
+    for j in range(0, k, 2):
         t, s = divmod(j, 8)
-        pivot_row = blocks[t][s : s + 1, :]
-        scaled = pivot_row * (1.0 / pivot_row[:, j : j + 1])
+        one, two = blocks[t][s : s + 1, :], blocks[t][s + 1 : s + 2, :]
+        cross = one[:, j + 1 : j + 2]
+        below = two[:, j : j + 1]
+        inverse_one = 1.0 / one[:, j : j + 1]
+        below = below * inverse_one
+        inverse_two = 1.0 / (two[:, j + 1 : j + 2] - below * cross)
+        scaled_one = one * inverse_one
+        scaled_two = (two - below * one) * inverse_two
+        cross = cross * inverse_one
         for i in range(t, k // 8):
-            factor = blocks[i][:, j : j + 1]
-            change = factor * scaled
+            left_one, left_two = blocks[i][:, j : j + 1], blocks[i][:, j + 1 : j + 2]
+            left_two = left_two - left_one * cross
+            change_one, change_two = left_one * scaled_one, left_two * scaled_two
             if i == t:
-                change = jnp.where(inner > s, change, 0.0)
-            blocks[i] = blocks[i] - change
-        if j == k // 2:
-            second = send(1, 1, receive(1, 0, second))
+                change_one = jnp.where(inner > s, change_one, 0.0)
+                change_two = jnp.where(inner > s + 1, change_two, 0.0)
+            blocks[i] = blocks[i] - change_one - change_two
+        if j == 3 * k // 4:
+            second = send(1, 2, receive(1, 1, second))
     whole = jnp.concatenate(blocks, axis=0)
     pivots = jnp.sum(jnp.where(lane == row, whole, 0.0), axis=1, keepdims=True)
     inverse = whole[:, start : start + k] / jnp.sqrt(pivots)
@@ -540,15 +575,25 @@
             )
             copy.start()
             stores.append(copy)
-        if z == nz // 2:
-            second = send(1, 2, receive(1, 1, second))
     middle = unfold(receive(1, 2, second))[:, 0:k]
     product = jnp.dot(inverse, middle, precision=HIGH, preferred_element_type=F32)
     product = lax.dot_general(product, inverse, NT, precision=HIGH, preferred_element_type=F32)
     projected[...] = product + jnp.where(lane[:, 0:k] == row[:, 0:k], 1.0, 0.0)
-    for copy in field_copies + probe_copies + tree + pending:
+    for copy in field_copies + probe_copies + [copy for copy, _, _ in tree] + pending:
         copy.wait_send()
     for copy in stores:
+        copy.wait()
+
+
+def copy_kernel(pieces, basis_in, projected_in, basis, projected, sem):
+    size = basis.shape[0] // pieces
+    copies = [pltpu.make_async_copy(projected_in, projected, sem.at[pieces])]
+    for i in range(pieces):
+        part = pl.ds(i * size, size)
+        copies.append(pltpu.make_async_copy(basis_in.at[part], basis.at[part], sem.at[i]))
+    for copy in copies:
+        copy.start()
+    for copy in copies:
         copy.wait()
 
 
@@ -635,7 +680,15 @@
         probes.reshape(k * lines, leaf), classes, class_table, weights, prior_block, prior_left,
         prior_right, block_ranks,
     )
-    return basis, projected
+    pieces = 16
+    return pl.pallas_call(
+        functools.partial(copy_kernel, pieces),
+        out_shape=(shape((k, nz, nx, leaf), F32), shape((k, k), F32)),
+        in_specs=[HBM] * 2,
+        out_specs=(HBM, HBM),
+        scratch_shapes=[dma((pieces + 1,))],
+        compiler_params=params(),
+    )(basis, projected)
 
 
 def solution(mesh):

time: 75.4 us -> 166 us (2.20)
  Pallas kernels: 69.9 us -> 166 us
  local copies, waits for them, and re-layouts: 4.72 us -> 0 us
    pallas_call x0 -> x1, Pallas kernels: none -> 97.3 us  [shards(): pl.pallas_call(functools.partial(copy_kernel, pieces), out_shape=(shape((...]
    unnamed x4 -> x0, local copies, waits for them, and re-layouts: 4.72 us -> none
where the time goes in v3:
time: 166 us
  Pallas kernels  166 us (100%)
    pallas_call x1, Pallas kernels, shards(): pl.pallas_call(functools.partial(copy_kernel, pieces), out_shape=(shape((...  97.3 us
    pallas_call x1, Pallas kernels, shards(): pl.pallas_call(functools.partial(sketch_kernel, ng, ny, k, nz, nx, levels...  68.4 us

profile of v3, /device:TPU:1, one launch (start us, length us, event | category | flops | bytes accessed | tf_op | source)
XLA Modules:
  0.0 166.3 jit_solution(5398950236472248107)
XLA Ops:
  0.6 68.4 %shard_map.95 = (f32[48,4,16,256]{3,2,1,0:T(8,128)}, f32[48,48]{1,0:T(8,128)}) custom-call(bf16[3072,256]{1,0:T(8,128)(2,1)} %bitcast.1, s32[4,16,256]{2,1,0:T(8,128)} %classes_in.1, f32[8]{0:T(128)} %table_in.1, f32[4,16,256]{2,1,0:T(8,128)} %weights_in.1, f32[256,256]{1,0:T(8,128)} %block_in.1, f32[8,16,256]{2,1,0:T(8,128)} %left_in.1, ...), custom_call_target="tpu_custom_call" | custom-call | tf_op jit(solution)/shard_map/pallas_call | solution.py:623
  69.0 97.3 %shard_map.96 = (f32[48,4,16,256]{3,2,1,0:T(8,128)}, f32[48,48]{1,0:T(8,128)}) custom-call(f32[48,4,16,256]{3,2,1,0:T(8,128)} %get-tuple-element.4.basis_in, f32[48,48]{1,0:T(8,128)} %get-tuple-element.5.projected_in), custom_call_target="tpu_custom_call" | custom-call | tf_op jit(solution)/shard_map/pallas_call | solution.py:684

commit v4 on v3

--- a/solution.py
+++ b/solution.py
@@ -34,12 +34,50 @@
     return copy
 
 
+def eliminate(blocks, t):
+    inner = lax.broadcasted_iota(jnp.int32, (8, LANES), 0)
+
+    def spread(value):
+        return jnp.broadcast_to(value, (8, LANES))
+
+    columns = [spread(blocks[t][:, 8 * t + c : 8 * t + c + 1]) for c in range(8)]
+    entry = [[spread(columns[c][r : r + 1, :]) for c in range(r + 1)] for r in range(8)]
+    rows = [spread(blocks[t][r : r + 1, :]) for r in range(8)]
+    factor = [[None] * 8 for _ in range(8)]
+    inverses = []
+    for q in range(8):
+        inverses.append(1.0 / entry[q][q])
+        for r in range(q + 1, 8):
+            factor[r][q] = entry[r][q] * inverses[q]
+        for r in range(q + 1, 8):
+            for c in range(q + 1, r + 1):
+                entry[r][c] = entry[r][c] - factor[r][q] * entry[c][q]
+    for r in range(8):
+        for q in range(r):
+            rows[r] = rows[r] - factor[r][q] * rows[q]
+    scaled = [rows[q] * inverses[q] for q in range(8)]
+    for i in range(t + 1, len(blocks)):
+        lefts = [spread(blocks[i][:, 8 * t + q : 8 * t + q + 1]) for q in range(8)]
+        for q in range(8):
+            for p in range(q):
+                lefts[q] = lefts[q] - lefts[p] * factor[q][p]
+        changes = [lefts[q] * scaled[q] for q in range(8)]
+        while len(changes) > 1:
+            changes = [changes[n] + changes[n + 1] for n in range(0, len(changes), 2)]
+        blocks[i] = blocks[i] - changes[0]
+    done, pivots = rows[0], entry[0][0]
+    for r in range(1, 8):
+        done = jnp.where(inner == r, rows[r], done)
+        pivots = jnp.where(inner == r, entry[r][r], pivots)
+    return done, 1.0 / jnp.sqrt(pivots)
+
+
 def sketch_kernel(
     ng, ny, k, nz, nx, levels, leaf, groups, cells,
     probes_in, classes_in, table_in, weights_in, block_in, left_in, right_in, ranks_in,
     out, projected,
     shl, buffer, store_sem, probes, classes, table, weights, block, left, right, ranks, load_sem,
-    pt, cond, pf, xh, hy, cx, cy, hs, cxs, cys, send_sem, recv_sem,
+    pt, cond, pf, xh, hy, hf, cx, cy, hs, cxs, cys, send_sem, recv_sem,
     ce, dg, dd, wd, fx, fyp, fym, fz, f1, a1, wt, acc, cuf, uc,
     trees, tree_send, tree_recv, packed, gathered, sum_send, sum_recv,
 ):
@@ -259,12 +297,9 @@
 
     def edge_tile(z, x, which):
         line = z * nx + x
-        above = hy[3 + which].astype(F32) * (has_x[which] * has_y[1])
-        below = hy[which].astype(F32) * (has_x[which] * has_y[0])
-        above = pltpu.roll(above, lax.rem(LANES - 2 * line + LANES, LANES), 1)
-        below = pltpu.roll(below, lax.rem(2 * LANES - 2 - 2 * line, LANES), 1)
-        value = jnp.where(tile_lane < 2, above, 0.0)
-        return jnp.where(tile_lane >= LANES - 2, below, value)
+        above = pltpu.roll(hf[3 + which], lax.rem(LANES - 2 * line + LANES, LANES), 1)
+        below = pltpu.roll(hf[which], lax.rem(2 * LANES - 2 - 2 * line, LANES), 1)
+        return jnp.where(tile_lane < LANES // 2, above, below)
 
     def inner_tiles(z, x, value):
         inverse = tiles(dd, z, x)
@@ -282,6 +317,10 @@
     lax.fori_loop(0, nx, forward_inner, 0)
     for copy in probe_copies[:6]:
         copy.wait_recv()
+
+    for which in range(3):
+        hf[which] = hy[which].astype(F32) * (has_x[which] * has_y[0])
+        hf[3 + which] = hy[3 + which].astype(F32) * (has_x[which] * has_y[1])
 
     def forward_edges(x, carry):
         for z in range(nz):
@@ -521,31 +560,13 @@
     start = LANES // 2
     whole = jnp.where(lane < k, matrix, jnp.where(lane == row + start, 1.0, 0.0))
     blocks = [whole[8 * t : 8 * t + 8] for t in range(k // 8)]
-    inner = lax.broadcasted_iota(jnp.int32, (8, LANES), 0)
-    for j in range(0, k, 2):
-        t, s = divmod(j, 8)
-        one, two = blocks[t][s : s + 1, :], blocks[t][s + 1 : s + 2, :]
-        cross = one[:, j + 1 : j + 2]
-        below = two[:, j : j + 1]
-        inverse_one = 1.0 / one[:, j : j + 1]
-        below = below * inverse_one
-        inverse_two = 1.0 / (two[:, j + 1 : j + 2] - below * cross)
-        scaled_one = one * inverse_one
-        scaled_two = (two - below * one) * inverse_two
-        cross = cross * inverse_one
-        for i in range(t, k // 8):
-            left_one, left_two = blocks[i][:, j : j + 1], blocks[i][:, j + 1 : j + 2]
-            left_two = left_two - left_one * cross
-            change_one, change_two = left_one * scaled_one, left_two * scaled_two
-            if i == t:
-                change_one = jnp.where(inner > s, change_one, 0.0)
-                change_two = jnp.where(inner > s + 1, change_two, 0.0)
-            blocks[i] = blocks[i] - change_one - change_two
-        if j == 3 * k // 4:
+    inverse = []
+    for t in range(k // 8):
+        done, scale = eliminate(blocks, t)
+        inverse.append(done[:, start : start + k] * scale[:, 0:k])
+        if t == k // 16:
             second = send(1, 2, receive(1, 1, second))
-    whole = jnp.concatenate(blocks, axis=0)
-    pivots = jnp.sum(jnp.where(lane == row, whole, 0.0), axis=1, keepdims=True)
-    inverse = whole[:, start : start + k] / jnp.sqrt(pivots)
+    inverse = jnp.concatenate(inverse, axis=0)
 
     high = inverse.astype(BF16)
     low = (inverse - high.astype(F32)).astype(BF16)
@@ -585,16 +606,26 @@
         copy.wait()
 
 
-def copy_kernel(pieces, basis_in, projected_in, basis, projected, sem):
+def copy_kernel(pieces, basis_in, projected_in, basis, projected, wide, small, load_sem, store_sem):
     size = basis.shape[0] // pieces
-    copies = [pltpu.make_async_copy(projected_in, projected, sem.at[pieces])]
-    for i in range(pieces):
-        part = pl.ds(i * size, size)
-        copies.append(pltpu.make_async_copy(basis_in.at[part], basis.at[part], sem.at[i]))
-    for copy in copies:
-        copy.start()
-    for copy in copies:
-        copy.wait()
+    parts = [pl.ds(i * size, size) for i in range(pieces)]
+    loads = [
+        pltpu.make_async_copy(basis_in.at[part], wide.at[part], load_sem.at[i])
+        for i, part in enumerate(parts)
+    ]
+    loads.insert(1, pltpu.make_async_copy(projected_in, small, load_sem.at[pieces]))
+    stores = [
+        pltpu.make_async_copy(wide.at[part], basis.at[part], store_sem.at[i])
+        for i, part in enumerate(parts)
+    ]
+    stores.insert(1, pltpu.make_async_copy(small, projected, store_sem.at[pieces]))
+    for load in loads:
+        load.start()
+    for load, store in zip(loads, stores):
+        load.wait()
+        store.start()
+    for store in stores:
+        store.wait()
 
 
 def params(**more):
@@ -648,6 +679,7 @@
             vmem((2, k * lines, LANES), F32),
             vmem((2, nz, 2, k, leaf), BF16),
             vmem((6, k, LANES), BF16),
+            vmem((6, k, LANES), F32),
             vmem((2, 4 * nz, leaf), F32),
             vmem((6, nx, LANES), F32),
             vmem((2, k, LANES), BF16),
@@ -680,13 +712,18 @@
         probes.reshape(k * lines, leaf), classes, class_table, weights, prior_block, prior_left,
         prior_right, block_ranks,
     )
-    pieces = 16
+    pieces = 8
     return pl.pallas_call(
         functools.partial(copy_kernel, pieces),
         out_shape=(shape((k, nz, nx, leaf), F32), shape((k, k), F32)),
         in_specs=[HBM] * 2,
         out_specs=(HBM, HBM),
-        scratch_shapes=[dma((pieces + 1,))],
+        scratch_shapes=[
+            vmem((k, nz, nx, leaf), F32),
+            vmem((k, k), F32),
+            dma((pieces + 1,)),
+            dma((pieces + 1,)),
+        ],
         compiler_params=params(),
     )(basis, projected)
 

time: 166 us -> 67.2 us (0.40)
  Pallas kernels: 166 us -> 66.1 us
    pallas_call x1, Pallas kernels: 97.3 us -> 2.81 us  [shards(): pl.pallas_call(functools.partial(copy_kernel, pieces), out_shape=(shape((...]
    pallas_call x1, Pallas kernels: 68.4 us -> 63.3 us  [shards(): pl.pallas_call(functools.partial(sketch_kernel, ng, ny, k, nz, nx, levels...]
where the time goes in v4:
time: 67.2 us; the launch traced here: 66.8 us
  Pallas kernels  66.1 us (98%)
    pallas_call x1, Pallas kernels, shards(): pl.pallas_call(functools.partial(sketch_kernel, ng, ny, k, nz, nx, levels...  63.3 us
    pallas_call x1, Pallas kernels, shards(): pl.pallas_call(functools.partial(copy_kernel, pieces), out_shape=(shape((...  2.81 us

profile of v4, /device:TPU:1, one launch (start us, length us, event | category | flops | bytes accessed | tf_op | source)
XLA Modules:
  0.0 66.8 jit_solution(14396642728142734579)
XLA Ops:
  0.6 63.3 %shard_map.95 = (f32[48,4,16,256]{3,2,1,0:T(8,128)}, f32[48,48]{1,0:T(8,128)}) custom-call(bf16[3072,256]{1,0:T(8,128)(2,1)} %bitcast.1, s32[4,16,256]{2,1,0:T(8,128)} %classes_in.1, f32[8]{0:T(128)} %table_in.1, f32[4,16,256]{2,1,0:T(8,128)} %weights_in.1, f32[256,256]{1,0:T(8,128)} %block_in.1, f32[8,16,256]{2,1,0:T(8,128)} %left_in.1, ...), custom_call_target="tpu_custom_call" | custom-call | tf_op jit(solution)/shard_map/pallas_call | solution.py:654
  64.0 2.8 %shard_map.96 = (f32[48,4,16,256]{3,2,1,0:T(8,128)}, f32[48,48]{1,0:T(8,128)}) custom-call(f32[48,4,16,256]{3,2,1,0:T(8,128)} %get-tuple-element.4.basis_in, f32[48,48]{1,0:T(8,128)} %get-tuple-element.5.projected_in), custom_call_target="tpu_custom_call" | custom-call | tf_op jit(solution)/shard_map/pallas_call | solution.py:716

commit v5 on v4

--- a/solution.py
+++ b/solution.py
@@ -108,8 +108,6 @@
         ([(gx, lax.rem(at_y + d, high_y) * pair + at_c) for d in range(1, high_y)], at_y),
     ]
     column = [(gx, lax.rem(gy + d, ny)) for d in range(1, ny)]
-    barrier, count = signal_all(around + stages[0][0] + stages[1][0] + column)
-
     loads = [
         pltpu.make_async_copy(source, target, load_sem.at[i])
         for i, (source, target) in enumerate(
@@ -127,6 +125,7 @@
     ]
     for load in loads:
         load.start()
+    barrier, count = signal_all(around + stages[0][0] + stages[1][0] + column)
 
     lines = nz * nx
     for load in loads[:3]:
@@ -157,41 +156,12 @@
     cys[0] = low
     cys[1] = high
 
-    loads[3].wait()
-    chunk = 512
-
-    def widen(i, carry):
-        rows = pl.ds(pl.multiple_of(i * chunk, chunk), chunk)
-        value = probes[rows, :].astype(F32)
-        pf[0, rows, :] = value[:, :LANES]
-        pf[1, rows, :] = value[:, LANES:]
-        return carry
-
-    lax.fori_loop(0, k * lines // chunk, widen, 0)
-
-    place = lax.broadcasted_iota(jnp.int32, (k, LANES), 1) // 2
-
-    def turn(line, carry):
-        low, high = carry
-        lo = pf[0, pl.ds(line, k, stride=lines), :]
-        hi = pf[1, pl.ds(line, k, stride=lines), :]
-        pt[line // nx, lax.rem(line, nx)] = jnp.concatenate([lo, hi], axis=1).astype(BF16)
-        low = jnp.where(place == line, pltpu.roll(lo, 2 * line, 1), low)
-        high = jnp.where(place == line, pltpu.roll(hi, lax.rem(2 * line + 2, LANES), 1), high)
-        return low, high
-
-    zero = jnp.zeros((k, LANES), F32)
-    low, high = lax.fori_loop(0, lines, turn, (zero, zero), unroll=4)
-    hs[0] = low.astype(BF16)
-    hs[1] = high.astype(BF16)
-
     pl.semaphore_wait(barrier, count)
     field_copies = [
         remote(cxs.at[1], cx.at[0], send_sem.at[2], recv_sem.at[2], (east, gy)),
         remote(cxs.at[0], cx.at[1], send_sem.at[3], recv_sem.at[3], (west, gy)),
     ]
     probe_copies = []
-    used = 4
     arrivals = [
         (side, which, row, column)
         for side, column in ((0, north), (1, south))
@@ -204,6 +174,34 @@
                 cys.at[1 - side], cy.at[slot], send_sem.at[4 + i], recv_sem.at[4 + i], (row, column)
             )
         )
+    loads[3].wait()
+    chunk = 512
+
+    def widen(i, carry):
+        rows = pl.ds(pl.multiple_of(i * chunk, chunk), chunk)
+        value = probes[rows, :].astype(F32)
+        pf[0, rows, :] = value[:, :LANES]
+        pf[1, rows, :] = value[:, LANES:]
+        return carry
+
+    lax.fori_loop(0, k * lines // chunk, widen, 0)
+
+    place = lax.broadcasted_iota(jnp.int32, (k, LANES), 1) // 2
+
+    def turn(line, carry):
+        low, high = carry
+        lo = pf[0, pl.ds(line, k, stride=lines), :]
+        hi = pf[1, pl.ds(line, k, stride=lines), :]
+        pt[line // nx, lax.rem(line, nx)] = jnp.concatenate([lo, hi], axis=1).astype(BF16)
+        low = jnp.where(place == line, pltpu.roll(lo, 2 * line, 1), low)
+        high = jnp.where(place == line, pltpu.roll(hi, lax.rem(2 * line + 2, LANES), 1), high)
+        return low, high
+
+    zero = jnp.zeros((k, LANES), F32)
+    low, high = lax.fori_loop(0, lines, turn, (zero, zero), unroll=4)
+    hs[0] = low.astype(BF16)
+    hs[1] = high.astype(BF16)
+
     for i, (side, which, row, column) in enumerate(arrivals):
         slot = side * 3 + which
         probe_copies.append(
@@ -365,8 +363,7 @@
 
     acc[...] = jnp.zeros_like(acc)
 
-    def finish(x, slot, apart):
-        whole_high, whole_low = [], []
+    def finish(x):
         for z in range(nz):
             centre, sums = near(a1, z, x, x + 1, 2)
             diagonal, inverse = tiles(dg, z, x), tiles(dd, z, x)
@@ -379,23 +376,24 @@
                 axis=1,
             )
             high = sketch.astype(BF16)
-            low = (sketch - high.astype(F32)).astype(BF16)
             shl[z * nx + x, 0:k, :] = high
-            shl[z * nx + x, k : 2 * k, :] = low
-            whole_high.append(high)
-            whole_low.append(low)
+            shl[z * nx + x, k : 2 * k, :] = (sketch - high.astype(F32)).astype(BF16)
+
+    def products(x, slot, apart):
+        whole = [shl[z * nx + x] for z in range(nz)]
         applied = lax.dot_general(
-            jnp.concatenate(whole_high, axis=0), wt[...], NT, preferred_element_type=F32
+            jnp.concatenate([part[0:k] for part in whole], axis=0),
+            wt[...],
+            NT,
+            preferred_element_type=F32,
         )
         rows = []
         for z in range(nz):
             part = applied[z * k : (z + 1) * k]
             cuf[slot + z * apart] = part[:, leaf:]
             rows.append(part[:, :leaf].astype(BF16))
-        high = jnp.concatenate(whole_high, axis=1)
-        low = jnp.concatenate(whole_low, axis=1)
-        lhs = jnp.concatenate([high, low], axis=0)
-        rhs = jnp.concatenate([high, low, jnp.concatenate(rows, axis=1)], axis=0)
+        lhs = jnp.concatenate(whole, axis=1)
+        rhs = jnp.concatenate([lhs, jnp.concatenate(rows, axis=1)], axis=0)
         acc[...] += lax.dot_general(lhs, rhs, NT, preferred_element_type=F32)
 
     lax.fori_loop(2, nx, adjoint, 0)
@@ -403,10 +401,13 @@
     early = nz * inner_rows // (LANES // rank)
 
     def finish_inner(x, carry):
-        finish(x, x - 2, inner_rows)
+        products(x - 1, x - 3, inner_rows)
+        finish(x)
         return carry
 
-    lax.fori_loop(2, nx - 2, finish_inner, 0)
+    finish(2)
+    lax.fori_loop(3, nx - 2, finish_inner, 0)
+    products(nx - 3, nx - 5, inner_rows)
 
     count = LANES // rank
     slot = tile_lane // rank
@@ -468,12 +469,18 @@
     def adjoint_outer(i, carry):
         return adjoint(jnp.where(i < 2, i, nx - 2 + i), carry)
 
+    def outer_row(i):
+        return jnp.where(i < 2, i, nx - 4 + i)
+
     def finish_outer(i, carry):
-        finish(jnp.where(i < 2, i, nx - 4 + i), nz * inner_rows + i, 4)
+        products(outer_row(i - 1), nz * inner_rows + i - 1, 4)
+        finish(outer_row(i))
         return carry
 
     lax.fori_loop(0, 4, adjoint_outer, 0)
-    lax.fori_loop(0, 4, finish_outer, 0)
+    finish(0)
+    lax.fori_loop(1, 4, finish_outer, 0)
+    products(nx - 1, nz * inner_rows + 3, 4)
 
     half_k, half_lanes = k // 2, LANES // 2
     half_lane = lax.broadcasted_iota(jnp.int32, (half_k, LANES), 1)
@@ -587,7 +594,7 @@
             buffer[z, 1, pl.ds(x, k, stride=nx), :] = value[:, LANES:]
             return carry
 
-        lax.fori_loop(0, nx, one, 0, unroll=4)
+        lax.fori_loop(0, nx, one, 0, unroll=8)
         for i in range(2):
             copy = pltpu.make_async_copy(
                 buffer.at[z, i].reshape(k, nx, LANES),

time: 67.2 us -> 69.1 us (1.028)
  Pallas kernels: 66.1 us -> 67.9 us
    pallas_call x1, Pallas kernels: 63.3 us -> 65.1 us  [shards(): pl.pallas_call(functools.partial(sketch_kernel, ng, ny, k, nz, nx, levels...]
where the time goes in v5:
time: 69.1 us; the launch traced here: 68.5 us
  Pallas kernels  67.9 us (98%)
    pallas_call x1, Pallas kernels, shards(): pl.pallas_call(functools.partial(sketch_kernel, ng, ny, k, nz, nx, levels...  65.1 us
    pallas_call x1, Pallas kernels, shards(): pl.pallas_call(functools.partial(copy_kernel, pieces), out_shape=(shape((...  2.81 us

profile of v5, /device:TPU:1, one launch (start us, length us, event | category | flops | bytes accessed | tf_op | source)
XLA Modules:
  0.0 68.5 jit_solution(17699477723148990966)
XLA Ops:
  0.6 65.1 %shard_map.95 = (f32[48,4,16,256]{3,2,1,0:T(8,128)}, f32[48,48]{1,0:T(8,128)}) custom-call(bf16[3072,256]{1,0:T(8,128)(2,1)} %bitcast.1, s32[4,16,256]{2,1,0:T(8,128)} %classes_in.1, f32[8]{0:T(128)} %table_in.1, f32[4,16,256]{2,1,0:T(8,128)} %weights_in.1, f32[256,256]{1,0:T(8,128)} %block_in.1, f32[8,16,256]{2,1,0:T(8,128)} %left_in.1, ...), custom_call_target="tpu_custom_call" | custom-call | tf_op jit(solution)/shard_map/pallas_call | solution.py:661
  65.7 2.8 %shard_map.96 = (f32[48,4,16,256]{3,2,1,0:T(8,128)}, f32[48,48]{1,0:T(8,128)}) custom-call(f32[48,4,16,256]{3,2,1,0:T(8,128)} %get-tuple-element.4.basis_in, f32[48,48]{1,0:T(8,128)} %get-tuple-element.5.projected_in), custom_call_target="tpu_custom_call" | custom-call | tf_op jit(solution)/shard_map/pallas_call | solution.py:723

commit v6 on v5

--- a/solution.py
+++ b/solution.py
@@ -156,12 +156,41 @@
     cys[0] = low
     cys[1] = high
 
+    loads[3].wait()
+    chunk = 512
+
+    def widen(i, carry):
+        rows = pl.ds(pl.multiple_of(i * chunk, chunk), chunk)
+        value = probes[rows, :].astype(F32)
+        pf[0, rows, :] = value[:, :LANES]
+        pf[1, rows, :] = value[:, LANES:]
+        return carry
+
+    lax.fori_loop(0, k * lines // chunk, widen, 0)
+
+    place = lax.broadcasted_iota(jnp.int32, (k, LANES), 1) // 2
+
+    def turn(line, carry):
+        low, high = carry
+        lo = pf[0, pl.ds(line, k, stride=lines), :]
+        hi = pf[1, pl.ds(line, k, stride=lines), :]
+        pt[line // nx, lax.rem(line, nx)] = jnp.concatenate([lo, hi], axis=1).astype(BF16)
+        low = jnp.where(place == line, pltpu.roll(lo, 2 * line, 1), low)
+        high = jnp.where(place == line, pltpu.roll(hi, lax.rem(2 * line + 2, LANES), 1), high)
+        return low, high
+
+    zero = jnp.zeros((k, LANES), F32)
+    low, high = lax.fori_loop(0, lines, turn, (zero, zero), unroll=4)
+    hs[0] = low.astype(BF16)
+    hs[1] = high.astype(BF16)
+
     pl.semaphore_wait(barrier, count)
     field_copies = [
         remote(cxs.at[1], cx.at[0], send_sem.at[2], recv_sem.at[2], (east, gy)),
         remote(cxs.at[0], cx.at[1], send_sem.at[3], recv_sem.at[3], (west, gy)),
     ]
     probe_copies = []
+    used = 4
     arrivals = [
         (side, which, row, column)
         for side, column in ((0, north), (1, south))
@@ -174,34 +203,6 @@
                 cys.at[1 - side], cy.at[slot], send_sem.at[4 + i], recv_sem.at[4 + i], (row, column)
             )
         )
-    loads[3].wait()
-    chunk = 512
-
-    def widen(i, carry):
-        rows = pl.ds(pl.multiple_of(i * chunk, chunk), chunk)
-        value = probes[rows, :].astype(F32)
-        pf[0, rows, :] = value[:, :LANES]
-        pf[1, rows, :] = value[:, LANES:]
-        return carry
-
-    lax.fori_loop(0, k * lines // chunk, widen, 0)
-
-    place = lax.broadcasted_iota(jnp.int32, (k, LANES), 1) // 2
-
-    def turn(line, carry):
-        low, high = carry
-        lo = pf[0, pl.ds(line, k, stride=lines), :]
-        hi = pf[1, pl.ds(line, k, stride=lines), :]
-        pt[line // nx, lax.rem(line, nx)] = jnp.concatenate([lo, hi], axis=1).astype(BF16)
-        low = jnp.where(place == line, pltpu.roll(lo, 2 * line, 1), low)
-        high = jnp.where(place == line, pltpu.roll(hi, lax.rem(2 * line + 2, LANES), 1), high)
-        return low, high
-
-    zero = jnp.zeros((k, LANES), F32)
-    low, high = lax.fori_loop(0, lines, turn, (zero, zero), unroll=4)
-    hs[0] = low.astype(BF16)
-    hs[1] = high.astype(BF16)
-
     for i, (side, which, row, column) in enumerate(arrivals):
         slot = side * 3 + which
         probe_copies.append(

time: 69.1 us -> 66.6 us (0.964)
  Pallas kernels: 67.9 us -> 65.3 us
    pallas_call x1, Pallas kernels: 65.1 us -> 62.5 us  [shards(): pl.pallas_call(functools.partial(sketch_kernel, ng, ny, k, nz, nx, levels...]
where the time goes in v6:
time: 66.6 us; the launch traced here: 66 us
  Pallas kernels  65.3 us (98%)
    pallas_call x1, Pallas kernels, shards(): pl.pallas_call(functools.partial(sketch_kernel, ng, ny, k, nz, nx, levels...  62.5 us
    pallas_call x1, Pallas kernels, shards(): pl.pallas_call(functools.partial(copy_kernel, pieces), out_shape=(shape((...  2.81 us

profile of v6, /device:TPU:1, one launch (start us, length us, event | category | flops | bytes accessed | tf_op | source)
XLA Modules:
  0.0 66.0 jit_solution(1564267771684087796)
XLA Ops:
  0.6 62.5 %shard_map.95 = (f32[48,4,16,256]{3,2,1,0:T(8,128)}, f32[48,48]{1,0:T(8,128)}) custom-call(bf16[3072,256]{1,0:T(8,128)(2,1)} %bitcast.1, s32[4,16,256]{2,1,0:T(8,128)} %classes_in.1, f32[8]{0:T(128)} %table_in.1, f32[4,16,256]{2,1,0:T(8,128)} %weights_in.1, f32[256,256]{1,0:T(8,128)} %block_in.1, f32[8,16,256]{2,1,0:T(8,128)} %left_in.1, ...), custom_call_target="tpu_custom_call" | custom-call | tf_op jit(solution)/shard_map/pallas_call | solution.py:662
  63.2 2.8 %shard_map.96 = (f32[48,4,16,256]{3,2,1,0:T(8,128)}, f32[48,48]{1,0:T(8,128)}) custom-call(f32[48,4,16,256]{3,2,1,0:T(8,128)} %get-tuple-element.4.basis_in, f32[48,48]{1,0:T(8,128)} %get-tuple-element.5.projected_in), custom_call_target="tpu_custom_call" | custom-call | tf_op jit(solution)/shard_map/pallas_call | solution.py:724

commit v7 on v6

--- a/solution.py
+++ b/solution.py
@@ -313,7 +313,7 @@
             inner_tiles(z, x, pt[z, x].astype(F32))
         return carry
 
-    lax.fori_loop(0, nx, forward_inner, 0)
+    lax.fori_loop(0, nx, forward_inner, 0, unroll=2)
     for copy in probe_copies[:6]:
         copy.wait_recv()
 
@@ -326,7 +326,7 @@
             edge_tiles(z, x, edge_tile(z, x, 1))
         return carry
 
-    lax.fori_loop(0, nx, forward_edges, 0)
+    lax.fori_loop(0, nx, forward_edges, 0, unroll=2)
     def near(ref, z, x, row, count):
         centre = split(ref[z, row])
         ahead = [pltpu.roll(part, LANES - 1, 1) for part in centre]
@@ -397,7 +397,7 @@
         rhs = jnp.concatenate([lhs, jnp.concatenate(rows, axis=1)], axis=0)
         acc[...] += lax.dot_general(lhs, rhs, NT, preferred_element_type=F32)
 
-    lax.fori_loop(2, nx, adjoint, 0)
+    lax.fori_loop(2, nx, adjoint, 0, unroll=2)
     inner_rows = nx - 4
     early = nz * inner_rows // (LANES // rank)
 
@@ -428,7 +428,7 @@
             uc[index, group] = parts[index].astype(BF16)
         return carry
 
-    lax.fori_loop(0, early, gather, 0)
+    lax.fori_loop(0, early, gather, 0, unroll=2)
 
     def flipped(bits):
         device = gy
@@ -528,7 +528,7 @@
     first = send(0, 0, fold(total))
     leafpart = value[0:k, 2 * k :] + value[k:, 2 * k :]
 
-    lax.fori_loop(early, groups, gather, 0)
+    lax.fori_loop(early, groups, gather, 0, unroll=2)
     for copy, ready, never in tree:
         if never:
             copy.start()

time: 66.6 us -> 65.1 us (0.977)
  Pallas kernels: 65.3 us -> 63.7 us
    pallas_call x1, Pallas kernels: 62.5 us -> 60.9 us  [shards(): pl.pallas_call(functools.partial(sketch_kernel, ng, ny, k, nz, nx, levels...]
where the time goes in v7:
time: 65.1 us; the launch traced here: 64.3 us
  Pallas kernels  63.7 us (98%)
    pallas_call x1, Pallas kernels, shards(): pl.pallas_call(functools.partial(sketch_kernel, ng, ny, k, nz, nx, levels...  60.9 us
    pallas_call x1, Pallas kernels, shards(): pl.pallas_call(functools.partial(copy_kernel, pieces), out_shape=(shape((...  2.81 us

profile of v7, /device:TPU:1, one launch (start us, length us, event | category | flops | bytes accessed | tf_op | source)
XLA Modules:
  0.0 64.3 jit_solution(3259677610141841419)
XLA Ops:
  0.6 60.9 %shard_map.95 = (f32[48,4,16,256]{3,2,1,0:T(8,128)}, f32[48,48]{1,0:T(8,128)}) custom-call(bf16[3072,256]{1,0:T(8,128)(2,1)} %bitcast.1, s32[4,16,256]{2,1,0:T(8,128)} %classes_in.1, f32[8]{0:T(128)} %table_in.1, f32[4,16,256]{2,1,0:T(8,128)} %weights_in.1, f32[256,256]{1,0:T(8,128)} %block_in.1, f32[8,16,256]{2,1,0:T(8,128)} %left_in.1, ...), custom_call_target="tpu_custom_call" | custom-call | tf_op jit(solution)/shard_map/pallas_call | solution.py:662
  61.5 2.8 %shard_map.96 = (f32[48,4,16,256]{3,2,1,0:T(8,128)}, f32[48,48]{1,0:T(8,128)}) custom-call(f32[48,4,16,256]{3,2,1,0:T(8,128)} %get-tuple-element.4.basis_in, f32[48,48]{1,0:T(8,128)} %get-tuple-element.5.projected_in), custom_call_target="tpu_custom_call" | custom-call | tf_op jit(solution)/shard_map/pallas_call | solution.py:724
